TPU v7x, 32 devices: a whole 2x2x4 slice. The times are simulated.
32 devices in a mesh: wide: 8 (over z, x), narrow: 4 (over y, core).
Axes of the slice: x: 2, y: 2, z: 4, core: 2. Of those that a mesh axis runs over, the one named last changes fastest.
Arguments:
- patches: bfloat16 [3200, 16384], P('wide', 'narrow')
- ln_gain: bfloat16 [4, 3200], P(None, 'wide'), may hold values from 0.5 to 1.5
- ln_bias: bfloat16 [4, 3200], P(None, 'wide'), may hold values from -3 to 3
- first_weight: bfloat16 [4, 3200, 6144], P(None, 'wide', 'narrow'), may hold values from -0.0546875 to 0.0546875
- first_bias: bfloat16 [6144], P('narrow'), may hold values from -3 to 3
- second_weight: bfloat16 [6144, 6144], P('wide', 'narrow'), may hold values from -0.078125 to 0.078125
- second_bias: bfloat16 [6144], P('wide'), may hold values from -3 to 3
- text_embeds: bfloat16 [6144, 5120], P('wide', 'narrow'), may hold values from -6 to 6
- vis_pos: int32 [4096], replicated, may hold values from 0 to 5119, as said below
Outputs:
- prompt_embeds: bfloat16 [6144, 5120], P('wide', 'narrow')
Inputs may be any that keep to these rules, and one draw needn't show every extreme that they name: vis_pos is strictly increasing and made of runs of 256 consecutive prompt rows, one run per tile in tile order; the first visual row is the first prompt row and the last visual row is the last prompt row.
All inputs are finite; a program needn't handle non-finite values.
Results may differ from a plain program's by a relative error of at most 0.012.
Values may be sent and summed in bfloat16 or wider, within the bound.
No kernel may reach another device: no remote copies, remote signals or barrier semaphores. Data moves between devices by JAX's collectives and lax.ppermute only.
A program may use at most 128 MiB of HBM per device.

v0:
```python
import jax
import jax.numpy as jnp
from jax import lax
from jax.sharding import PartitionSpec as P

D = 3200
TILE_SIDE = 32


def shards(
    patches,
    ln_gain,
    ln_bias,
    first_weight,
    first_bias,
    second_weight,
    second_bias,
    text_embeds,
    vis_pos,
):
    half_side = TILE_SIDE // 2
    columns = patches.shape[0]
    local_rows = patches.reshape(columns, -1, half_side, 2, half_side, 2).transpose(
        3, 5, 0, 1, 2, 4
    )
    local_rows = local_rows.reshape(4, columns, -1)
    entries = 4.0 * D
    group_block = lax.all_to_all(local_rows, "wide", split_axis=2, concat_axis=1, tiled=True)
    own_rows = lax.all_gather(group_block, "narrow", axis=2, tiled=True)
    narrow_count = lax.axis_size("narrow")
    wide_count = lax.axis_size("wide")
    order_pos = vis_pos.reshape(narrow_count, wide_count, -1).transpose(1, 0, 2).reshape(-1)
    float_rows = own_rows.astype(jnp.float32)
    row_mean = jnp.sum(float_rows, axis=(0, 1)) / entries
    row_var = jnp.sum(float_rows * float_rows, axis=(0, 1)) / entries - row_mean * row_mean
    inverse = lax.rsqrt(row_var + 1e-05)
    weight_piece = lax.all_gather(first_weight, "wide", axis=1, tiled=True)
    gain_piece = lax.all_gather(ln_gain, "wide", axis=1, tiled=True)
    shift_piece = lax.all_gather(ln_bias, "wide", axis=1, tiled=True)
    normed = (
        (float_rows - row_mean[None, None, :])
        * inverse[None, None, :]
        * gain_piece.astype(jnp.float32)[:, :, None]
        + shift_piece.astype(jnp.float32)[:, :, None]
    ).astype(jnp.bfloat16)
    preact = jnp.einsum("scm,sce->me", normed, weight_piece, preferred_element_type=jnp.float32)
    activated = jax.nn.gelu(preact + first_bias.astype(jnp.float32), approximate=False).astype(
        jnp.bfloat16
    )
    partial_value = lax.dot_general(
        second_weight,
        lax.all_gather(activated, "wide", axis=0, tiled=True),
        (((1,), (1,)), ((), ())),
        preferred_element_type=jnp.float32,
    )
    prompt_rows = text_embeds.shape[1]
    first_row = lax.axis_index("narrow") * prompt_rows
    inside = (order_pos >= first_row) & (order_pos < first_row + prompt_rows)
    target = jnp.where(inside, order_pos - first_row, prompt_rows)
    bias_column = second_bias.astype(jnp.float32)[:, None]
    whole_prompt = prompt_rows * lax.axis_size("narrow")
    placed_term = (
        jnp.zeros((partial_value.shape[0], whole_prompt), jnp.float32)
        .at[:, order_pos]
        .set(partial_value)
    )
    summed = lax.psum_scatter(placed_term, "narrow", scatter_dimension=1, tiled=True)
    visual_mark = jnp.zeros((prompt_rows,), jnp.int32).at[target].set(1, mode="drop")
    visual_cols = (summed + bias_column).astype(jnp.bfloat16)
    return jnp.where(visual_mark[None, :] > 0, visual_cols, text_embeds)


def solution(mesh):
    in_specs = (
        P("wide", "narrow"),
        P(None, "wide"),
        P(None, "wide"),
        P(None, "wide", "narrow"),
        P("narrow"),
        P("wide", "narrow"),
        P("wide"),
        P("wide", "narrow"),
        P(),
    )
    out_specs = P("wide", "narrow")
    return jax.shard_map(shards, mesh=mesh, in_specs=in_specs, out_specs=out_specs, check_vma=False)
```

profile of v0, /device:TPU:1, one launch (start us, length us, event | category | flops | bytes accessed | tf_op | source)
XLA Modules:
  0.0 1351.8 jit_solution(4385029504259053902)
XLA Ops:
  6.5 6.1 copy.43
  12.7 7.4 reshape.103
  20.0 3.2 copy.44
  23.2 3.2 copy.45
  26.5 98.6 %all_to_all.18 = bf16[4,400,1024]{1,0,2:T(4,128)(2,1)} all-to-all(bf16[4,400,1024]{1,0,2:T(4,128)(2,1)S(1)} %copy.45), channel_id=1, replica_groups=mesh['wide'=8,'narrow'=4] {'wide'}, dimensions={2} | all-to-all | bytes 6553600 | tf_op jit(solution)/shard_map/all_to_all | solution.py:28
  125.0 7.7 copy.55
  132.7 0.0 all-gather.6.cloned.1.call-update
  132.8 0.0 copy-start.3
  132.8 0.0 copy-start.4
  132.8 0.0 all-gather.8.cloned.1.call-start
  132.8 0.7 all-gather.8.cloned.1.call-update
  133.5 0.0 all-gather.10.cloned.1.call-start
  133.6 24.0 %all-gather = bf16[8,400,4]{1,2,0:T(4,128)(2,1)S(1)} all-gather(bf16[1,400,4]{1,2,0:T(4,128)(2,1)S(1)} %bitcast.46), channel_id=1, replica_groups=mesh['wide'=8,'narrow'=4] {'wide'}, dimensions={0}, use_global_device_ids=true | all-gather | bytes 28800 | tf_op jit(solution)/shard_map/all_gather | solution.py:38
  157.6 0.1 reshape.125
  157.8 24.0 %all-gather.1 = bf16[8,400,4]{1,2,0:T(4,128)(2,1)S(1)} all-gather(bf16[1,400,4]{1,2,0:T(4,128)(2,1)S(1)} %bitcast.47), channel_id=1, replica_groups=mesh['wide'=8,'narrow'=4] {'wide'}, dimensions={0}, use_global_device_ids=true | all-gather | bytes 28800 | tf_op jit(solution)/shard_map/all_gather | solution.py:39
  181.8 0.1 reshape.126
  182.0 38.3 %all-gather.6.cloned.1.call-done = bf16[4,3200,512]{2,1,0:T(8,128)(2,1)} async-done(((bf16[4,3200,128]{2,1,0:T(8,128)(2,1)}), bf16[4,3200,512]{2,1,0:T(8,128)(2,1)}) %all-gather.6.cloned.1.call-update) | async-done | bytes 13107216 | tf_op jit(solution)/shard_map/all_gather | solution.py:29
  220.3 8.2 convert_reduce_fusion
  228.5 738.8 %all-gather.8.cloned.1.call-done = bf16[4,3200,1536]{2,1,0:T(8,128)(2,1)} async-done(((bf16[4,400,1536]{2,1,0:T(8,128)(2,1)}), bf16[4,3200,1536]{2,1,0:T(8,128)(2,1)}) %all-gather.8.cloned.1.call-update) | async-done | bytes 39321616 | tf_op jit(solution)/shard_map/all_gather | solution.py:37
  967.3 34.2 %fusion.21 = bf16[512,1536]{1,0:T(8,128)(2,1)} fusion(bf16[4,3200,1536]{2,1,0:T(8,128)(2,1)} %all-gather.8.cloned.1.call-done, bf16[4,3200,512]{2,1,0:T(8,128)(2,1)} %all-gather.6.cloned.1.call-done, f32[4,3200]{1,0:T(4,128)S(1)} %bitcast.42, f32[4,3200]{1,0:T(4,128)S(1)} %bitcast.41, f32[512]{0:T(512)S(1)} %get-tuple-element.10, ...), kind=kOutput, calls=%fused_computation.23 | convolution fusion | flops 20223885312 | bytes 54114304 | tf_op jit(solution)/shard_map/scm,sce->me/dot_general | solution.py:46
  1001.6 0.0 all-gather.10.cloned.1.call-update
  1001.6 0.0 reduce-scatter.2.cloned.1.call-start
  1001.7 0.1 compare_select_fusion.1
  1001.7 176.0 %all-gather.10.cloned.1.call-done = bf16[4096,1536]{1,0:T(8,128)(2,1)} async-done(((bf16[512,1536]{1,0:T(8,128)(2,1)}), bf16[4096,1536]{1,0:T(8,128)(2,1)}) %all-gather.10.cloned.1.call-update) | async-done | bytes 12582928 | tf_op jit(solution)/shard_map/all_gather | solution.py:52
  1177.8 15.7 %fusion.34 = f32[4096,768]{1,0:T(8,128)} fusion(bf16[4096,1536]{1,0:T(8,128)(2,1)} %all-gather.10.cloned.1.call-done, bf16[768,1536]{1,0:T(8,128)(2,1)S(1)} %copy-done), kind=kOutput, calls=%fused_computation.50 | convolution fusion | flops 9663676416 | bytes 27525120 | tf_op jit(solution)/shard_map/dot_general | solution.py:50
  1193.5 24.7 %scatter_custom_fusion.1 = f32[768,5120]{0,1:T(8,128)} fusion(s32[4096]{0:T(1024)S(1)} %bitcast.44, f32[4096,768]{1,0:T(8,128)} %fusion.34, f32[]{:T(128)} %constant.41.clone.1), kind=kCustom, calls=%fused_computation.15 | custom fusion | bytes 15729152 | tf_op jit(solution)/shard_map/scatter | solution.py:65
  1218.1 0.0 reduce-scatter.2.cloned.1.call-update
  1218.2 4.0 copy.51
  1222.1 15.5 %scatter_custom_fusion = s32[1280]{0:T(1024)S(1)} fusion(s32[4096]{0:T(1024)S(1)} %bitcast.43, s32[4096]{0:T(1024)S(1)} %broadcast.91, s32[]{:T(128)} %constant.37.clone.1), kind=kCustom, calls=%fused_computation.46 | custom fusion | bytes 5124 | tf_op jit(solution)/shard_map/scatter | solution.py:68
  1237.7 99.1 %reduce-scatter.2.cloned.1.call-done = f32[768,1280]{0,1:T(8,128)} async-done(((f32[768,5120]{0,1:T(8,128)}), f32[768,1280]{0,1:T(8,128)}) %reduce-scatter.2.cloned.1.call-update) | async-done | bytes 3932176 | tf_op jit(solution)/shard_map/reduce_scatter | solution.py:67
  1336.8 4.6 fusion.31
  1341.3 4.0 copy.52
  (19 shorter events, 0.1 us)
Async XLA Ops:
  6.5 1171.2 %copy-start = (bf16[768,1536]{1,0:T(8,128)(2,1)S(1)}, bf16[768,1536]{1,0:T(8,128)(2,1)}, u32[]{:S(2)}) copy-start(bf16[768,1536]{1,0:T(8,128)(2,1)} %param.14) | copy-start | bytes 7077892
  6.5 213.8 %all-gather.6.cloned.1.call-start = ((), (), s32[]{:S(2)}) async-start(), calls=%async_computation.2 | async-start | bytes 16384000 | tf_op jit(solution)/shard_map/all_gather | solution.py:29
  132.7 0.8 copy-start.2
  132.8 25.0 %copy-start.3 = (bf16[4,400]{1,0:T(4,128)(2,1)S(1)}, bf16[4,400]{1,0:T(4,128)(2,1)}, u32[]{:S(2)}) copy-start(bf16[4,400]{1,0:T(4,128)(2,1)} %param.11) | copy-start | bytes 9604
  132.8 49.2 %copy-start.4 = (bf16[1536]{0:T(1024)(128)(2,1)S(1)}, bf16[1536]{0:T(1024)(128)(2,1)}, u32[]{:S(2)}) copy-start(bf16[1536]{0:T(1024)(128)(2,1)} %param.13) | copy-start | bytes 9220
  132.8 834.6 %all-gather.8.cloned.1.call-start = ((), (), s32[]{:S(2)}) async-start(), calls=%async_computation.3 | async-start | bytes 44236800 | tf_op jit(solution)/shard_map/all_gather | solution.py:37
  133.5 1044.2 %all-gather.10.cloned.1.call-start = ((), (), s32[]{:S(2)}) async-start(), calls=%async_computation.4 | async-start | bytes 14155776 | tf_op jit(solution)/shard_map/all_gather | solution.py:52
  967.3 34.3 %copy-start.1 = (s32[4096]{0:T(1024)S(1)}, s32[4096]{0:T(1024)}, u32[]{:S(2)}) copy-start(s32[4096]{0:T(1024)} %param.17) | copy-start | bytes 49156
  1001.6 335.2 %reduce-scatter.2.cloned.1.call-start = ((), (), s32[]{:S(2)}) async-start(), calls=%async_computation.5 | async-start | bytes 19660800 | tf_op jit(solution)/shard_map/reduce_scatter | solution.py:67
  1218.2 4.0 copy-start.5
Sparse Core Ops, SparseCore 0:
  132.9 87.4 all-gather.5
  221.9 745.4 all-gather.7
  1001.7 175.9 all-gather.9
  1218.3 118.4 reduce-scatter.1
where the time goes:
time: 1350 us
  waiting for transfers between devices  1050 us (78%)
  blocking collectives  147 us (11%)
  local copies, waits for them, and re-layouts  76 us (6%)
  matrix products  49.9 us (4%)
    all_gather x1, waiting for transfers between devices, shards(): weight_piece = lax.all_gather(first_weight, 'wide', axis=1, tiled=True)  739 us
    all_gather x1, waiting for transfers between devices, shards(): lax.all_gather(activated, 'wide', axis=0, tiled=True)  176 us
    reduce_scatter x1, waiting for transfers between devices, shards(): lax.psum_scatter(placed_term, 'narrow', scatter_dimension=1, tiled=True)  99.1 us
    all_to_all x1, blocking collectives, shards(): lax.all_to_all(local_rows, 'wide', split_axis=2, concat_axis=1, tiled=True)  98.6 us
    all_gather x1, waiting for transfers between devices, shards(): own_rows = lax.all_gather(group_block, 'narrow', axis=2, tiled=True)  38.3 us
    dot_general x1, matrix products, shards(): jnp.einsum('scm,sce->me', normed, weight_piece, preferred_element_type=jn...  34.2 us
  transfers between devices with their start and end apart: 4, of which 4 were waited for; matrix products, arithmetic and copies ran while one was open for 2% of the time, Pallas kernels for 0%

commit v1 on v0

v1 whole, which is shorter than its diff:
```python
import jax
import jax.numpy as jnp
from jax import lax
from jax.experimental import pallas as pl
from jax.experimental.pallas import tpu as pltpu
from jax.sharding import PartitionSpec as P

D = 3200
TILE_SIDE = 32
TILE_ROWS = 256
HALF = 128
COLS = 512
F32 = jnp.float32
BF16 = jnp.bfloat16


def bit_reversed(bits):
    return [sum(((p >> b) & 1) << (bits - 1 - b) for b in range(bits)) for p in range(1 << bits)]


def swap(value, axis, mask):
    count = lax.axis_size(axis)
    return lax.ppermute(value, axis, [(i, i ^ mask) for i in range(count)])


def merge_kernel(patch_ref, order_ref, merged_ref, stats_ref):
    mixed = jnp.dot(patch_ref[...], order_ref[...], preferred_element_type=F32)
    total = jnp.zeros((1, HALF), F32)
    squares = jnp.zeros((1, HALF), F32)
    for slot in range(4):
        part = mixed[:, slot * HALF : (slot + 1) * HALF]
        merged_ref[0, slot] = part.astype(BF16)
        total += jnp.sum(part, axis=0, keepdims=True)
        squares += jnp.sum(part * part, axis=0, keepdims=True)
    stats_ref[0:1, :] = total
    stats_ref[1:2, :] = squares


def merge(patches):
    columns, width = patches.shape
    steps = width // COLS
    side = TILE_SIDE // 2
    source = lax.broadcasted_iota(jnp.int32, (COLS, COLS), 0)
    target = lax.broadcasted_iota(jnp.int32, (COLS, COLS), 1)
    slot = target // HALF
    row = target % HALF
    wanted = (
        (row // side) * (4 * side) + (slot // 2) * (2 * side) + (row % side) * 2 + slot % 2
    )
    order = (source == wanted).astype(BF16)
    return pl.pallas_call(
        merge_kernel,
        grid=(steps,),
        in_specs=[
            pl.BlockSpec((columns, COLS), lambda i: (0, i)),
            pl.BlockSpec((COLS, COLS), lambda i: (0, 0)),
        ],
        out_specs=[
            pl.BlockSpec((1, 4, columns, HALF), lambda i: (i, 0, 0, 0)),
            pl.BlockSpec((2, HALF), lambda i: (0, i)),
        ],
        out_shape=[
            jax.ShapeDtypeStruct((steps, 4, columns, HALF), BF16),
            jax.ShapeDtypeStruct((2, steps * HALF), F32),
        ],
        compiler_params=pltpu.CompilerParams(vmem_limit_bytes=32 * 1024 * 1024),
    )(patches, order)


def shards(
    patches,
    ln_gain,
    ln_bias,
    first_weight,
    first_bias,
    second_weight,
    second_bias,
    text_embeds,
    vis_pos,
):
    wide = lax.axis_size("wide")
    narrow = lax.axis_size("narrow")
    wide_bits = wide.bit_length() - 1
    narrow_bits = narrow.bit_length() - 1
    wide_at = lax.axis_index("wide")
    narrow_at = lax.axis_index("narrow")
    side_at = wide_at % 2
    column_at = wide_at // 2
    columns = patches.shape[0]
    hidden = first_weight.shape[2]
    features = second_weight.shape[0]
    tiles = patches.shape[1] // (4 * TILE_ROWS)
    prompt_rows = text_embeds.shape[1]
    depth = 4 * columns

    unit_order = bit_reversed(wide_bits - 1)
    block = hidden // len(unit_order)
    starts = [(q ^ column_at) * block for q in unit_order]
    flat_weight = first_weight.reshape(depth, hidden)
    first = jnp.concatenate(
        [lax.dynamic_slice_in_dim(flat_weight, s, block, 1).T for s in starts], axis=0
    )
    own_bias = lax.dynamic_slice_in_dim(first_bias, starts[0], block, 0).astype(F32)[:, None]
    second_own = jnp.concatenate(
        [lax.dynamic_slice_in_dim(second_weight, s, block, 1) for s in starts], axis=1
    )
    second_other = swap(second_own, "wide", 1)
    second = jnp.concatenate([second_other, second_own], axis=0)
    out_bias = jnp.concatenate([swap(second_bias, "wide", 1), second_bias]).astype(F32)[:, None]

    merged, stats = merge(patches)
    for bit in range(wide_bits):
        stats = stats + swap(stats, "wide", 1 << bit)
    entries = 4.0 * D
    row_mean = stats[0] / entries
    row_var = stats[1] / entries - row_mean * row_mean
    inverse = lax.rsqrt(row_var + 1e-05)
    gain = ln_gain.astype(F32)[:, :, None]
    shift = ln_bias.astype(F32)[:, :, None]

    def normed(half):
        values = lax.dynamic_index_in_dim(merged, half, 0, keepdims=False).astype(F32)
        mean = lax.dynamic_slice_in_dim(row_mean, half * HALF, HALF, 0)
        scale = lax.dynamic_slice_in_dim(inverse, half * HALF, HALF, 0)
        result = (values - mean[None, None, :]) * scale[None, None, :] * gain + shift
        return result.astype(BF16).reshape(depth, HALF)

    tile_order = bit_reversed(narrow_bits)

    def gathered(own):
        found = {0: own}
        for bit in reversed(range(narrow_bits)):
            for d in list(found):
                found[d ^ (1 << bit)] = swap(found[d], "narrow", 1 << bit)
        return jnp.concatenate([found[d] for d in tile_order], axis=1)

    finals = []
    for tile in range(tiles):
        theirs = gathered(normed(2 * tile + 1 - side_at))
        mine = gathered(normed(2 * tile + side_at))
        sent = jnp.dot(first, theirs, preferred_element_type=F32).astype(BF16)
        came = swap(sent, "wide", 1)
        total = jnp.dot(first, mine, preferred_element_type=F32) + came.astype(F32)
        for bit in range(1, wide_bits):
            total = total.astype(BF16)
            cut = total.shape[0] // 2
            came = swap(total[cut:], "wide", 1 << bit)
            total = total[:cut].astype(F32) + came.astype(F32)
        activated = jax.nn.gelu(total + own_bias, approximate=False).astype(BF16)
        pieces = [activated]
        for bit in reversed(range(1, wide_bits)):
            pieces = pieces + [swap(piece, "wide", 1 << bit) for piece in pieces]
        units = jnp.concatenate(pieces, axis=0)
        value = jnp.dot(second, units, preferred_element_type=F32)
        for bit in range(narrow_bits):
            value = value.astype(BF16)
            cut = value.shape[1] // 2
            came = swap(value[:, cut:], "narrow", 1 << bit)
            value = value[:, :cut].astype(F32) + came.astype(F32)
        visual = (value + out_bias).astype(BF16)
        other = swap(visual[:features], "wide", 1)
        finals.append(jnp.concatenate([visual[features:], other], axis=1))

    text_rows = narrow * prompt_rows - vis_pos.shape[0]
    first_row = narrow_at * prompt_rows
    half_rows = jnp.arange(HALF, dtype=jnp.int32)
    in_tile = jnp.concatenate([half_rows + side_at * HALF, half_rows + (1 - side_at) * HALF])
    placed, spots = [], []
    for step in range(1 - narrow, narrow):
        for tile in range(tiles):
            pairs = []
            for source in range(narrow):
                target = source + step
                low = (source * tiles + tile) * TILE_ROWS
                if (
                    0 <= target < narrow
                    and low < (target + 1) * prompt_rows
                    and low + text_rows + TILE_ROWS > target * prompt_rows
                ):
                    pairs.append((source, target))
            if not pairs:
                continue
            placed.append(finals[tile] if step == 0 else lax.ppermute(finals[tile], "narrow", pairs))
            whose = narrow_at - step
            at = (jnp.clip(whose, 0, narrow - 1) * tiles + tile) * TILE_ROWS
            spot = lax.dynamic_slice_in_dim(vis_pos, at, TILE_ROWS, 0)[in_tile] - first_row
            spots.append(jnp.where((whose >= 0) & (whose < narrow), spot, -1))
    spot = jnp.concatenate(spots)
    grid = jnp.arange(prompt_rows, dtype=jnp.int32)[None, :]
    hits = spot[:, None] == grid
    marked = jnp.any(hits, axis=0)
    moved = jnp.dot(
        jnp.concatenate(placed, axis=1), hits.astype(BF16), preferred_element_type=F32
    ).astype(BF16)
    return jnp.where(marked[None, :], moved, text_embeds)


def solution(mesh):
    in_specs = (
        P("wide", "narrow"),
        P(None, "wide"),
        P(None, "wide"),
        P(None, "wide", "narrow"),
        P("narrow"),
        P("wide", "narrow"),
        P("wide"),
        P("wide", "narrow"),
        P(),
    )
    out_specs = P("wide", "narrow")
    return jax.shard_map(shards, mesh=mesh, in_specs=in_specs, out_specs=out_specs, check_vma=False)
```

time: 1350 us -> 518 us (0.38)
  waiting for transfers between devices: 1050 us -> 292 us
  blocking collectives: 147 us -> 0 us
  starting transfers between devices: 0.12 us -> 101 us
  local copies, waits for them, and re-layouts: 76 us -> 33.6 us
  other arithmetic: 12.8 us -> 34.6 us
    all_gather x3 -> x0, waiting for transfers between devices: 953 us -> none  [the longest x1 739 us: shards(): weight_piece = lax.all_gather(first_weight, 'wide', axis=1, tiled=True)]
    ppermute x0 -> x71, waiting for transfers between devices: none -> 292 us  [the longest x65 283 us: swap(): return lax.ppermute(value, axis, [(i, i ^ mask) for i in range(count)])]
    ppermute x0 -> x71, starting transfers between devices: none -> 101 us  [the longest x65 88.2 us: swap(): return lax.ppermute(value, axis, [(i, i ^ mask) for i in range(count)])]
    reduce_scatter x1 -> x0, waiting for transfers between devices: 99.1 us -> none  [shards(): lax.psum_scatter(placed_term, 'narrow', scatter_dimension=1, tiled=True)]
    all_to_all x1 -> x0, blocking collectives: 98.6 us -> none  [shards(): lax.all_to_all(local_rows, 'wide', split_axis=2, concat_axis=1, tiled=True)]
    all_gather x2 -> x0, blocking collectives: 48.1 us -> none  [the longest x1 24 us: shards(): gain_piece = lax.all_gather(ln_gain, 'wide', axis=1, tiled=True)]
    scatter x2 -> x0, local copies, waits for them, and re-layouts: 40.2 us -> none  [the longest x1 24.7 us: shards(): placed_term = jnp.zeros((partial_value.shape[0], whole_prompt), jnp.float...]
    gather x0 -> x10, local copies, waits for them, and re-layouts: none -> 20.7 us  [shards(): lax.dynamic_slice_in_dim(vis_pos, at, TILE_ROWS, 0)[in_tile] - first_row]
  transfers between devices with their start and end apart: 4 -> 71, of which waited for: 4 -> 28; matrix products, arithmetic and copies ran while one was open for 2% -> 20% of each run, Pallas kernels for 0% -> 0%
where the time goes in v1:
time: 518 us; the launch traced here: 512 us
  waiting for transfers between devices  292 us (56%)
  starting transfers between devices  101 us (19%)
  matrix products  46.4 us (9%)
  other arithmetic  34.6 us (7%)
  local copies, waits for them, and re-layouts  33.6 us (6%)
    ppermute x65, waiting for transfers between devices, swap(): return lax.ppermute(value, axis, [(i, i ^ mask) for i in range(count)])  283 us
    ppermute x65, starting transfers between devices, swap(): return lax.ppermute(value, axis, [(i, i ^ mask) for i in range(count)])  88.2 us
    gather x10, local copies, waits for them, and re-layouts, shards(): lax.dynamic_slice_in_dim(vis_pos, at, TILE_ROWS, 0)[in_tile] - first_row  20.7 us
    dot_general x4, matrix products, shards(): sent = jnp.dot(first, theirs, preferred_element_type=F32).astype(BF16)  14.7 us
    dot_general x4, matrix products, shards(): total = jnp.dot(first, mine, preferred_element_type=F32) + came.astype(F32)  12.9 us
    ppermute x6, starting transfers between devices, shards(): lax.ppermute(finals[tile], 'narrow', pairs)  12.6 us
    unnamed x10, other arithmetic  11.6 us
    dot_general x4, matrix products, shards(): value = jnp.dot(second, units, preferred_element_type=F32)  10.8 us
  transfers between devices with their start and end apart: 71, of which 28 were waited for; matrix products, arithmetic and copies ran while one was open for 20% of the time, Pallas kernels for 0%

profile of v1, /device:TPU:1, one launch (start us, length us, event | category | flops | bytes accessed | tf_op | source)
XLA Modules:
  0.0 512.3 jit_solution(9336040853804994658)
XLA Ops:
  2.1 3.4 shard_map.91
  22.5 3.5 collective-permute-start.57
  29.0 5.6 %collective-permute-start.58 = (bf16[1600,128]{1,0:T(8,128)(2,1)}, bf16[1600,128]{1,0:T(8,128)(2,1)}, u32[]{:S(2)}, u32[]{:S(2)}) collective-permute-start(bf16[1600,128]{1,0:T(8,128)(2,1)} %collective-permute-done.56), channel_id=1, source_target_pairs={{0,1},{1,0},{2,3},{3,2},{4,5},{5,4},{6,7},{7,6},{8,9},{9,8},{10,11... | collective-permute-start | bytes 1228808 | tf_op jit(solution)/shard_map/ppermute | solution.py:23
  56.0 4.4 convolution_convert_fusion.1
  60.6 13.1 %collective-permute-done.40 = bf16[1600,128]{1,0:T(8,128)(2,1)S(1)} collective-permute-done((bf16[1600,128]{1,0:T(8,128)(2,1)S(1)}, bf16[1600,128]{1,0:T(8,128)(2,1)S(1)}, u32[]{:S(2)}, u32[]{:S(2)}) %collective-permute-start.40) | collective-permute-done | bytes 409632 | tf_op jit(solution)/shard_map/ppermute | solution.py:23
  76.0 4.1 convolution_convert_fusion.5
  80.2 3.9 collective-permute-done.7
  95.6 4.4 collective-permute-done.21
  102.6 18.9 %collective-permute-done.59 = bf16[1536,512]{1,0:T(8,128)(2,1)S(1)} collective-permute-done((bf16[1536,512]{1,0:T(8,128)(2,1)S(1)}, bf16[1536,512]{1,0:T(8,128)(2,1)S(1)}, u32[]{:S(2)}, u32[]{:S(2)}) %collective-permute-start.59) | collective-permute-done | bytes 1572896 | tf_op jit(solution)/shard_map/ppermute | solution.py:23
  122.1 3.5 fusion.7
  128.8 26.5 %collective-permute-done.27 = bf16[1536,512]{1,0:T(8,128)(2,1)S(1)} collective-permute-done((bf16[1536,512]{1,0:T(8,128)(2,1)S(1)}, bf16[1536,512]{1,0:T(8,128)(2,1)S(1)}, u32[]{:S(2)}, u32[]{:S(2)}) %collective-permute-start.27) | collective-permute-done | bytes 1572896 | tf_op jit(solution)/shard_map/ppermute | solution.py:23
  161.8 27.2 %collective-permute-done.43 = bf16[1536,512]{1,0:T(8,128)(2,1)S(1)} collective-permute-done((bf16[1536,512]{1,0:T(8,128)(2,1)S(1)}, bf16[1536,512]{1,0:T(8,128)(2,1)S(1)}, u32[]{:S(2)}, u32[]{:S(2)}) %collective-permute-start.43) | collective-permute-done | bytes 1572896 | tf_op jit(solution)/shard_map/ppermute | solution.py:23
  195.1 27.6 %collective-permute-done.10 = bf16[1536,512]{1,0:T(8,128)(2,1)S(1)} collective-permute-done((bf16[1536,512]{1,0:T(8,128)(2,1)S(1)}, bf16[1536,512]{1,0:T(8,128)(2,1)S(1)}, u32[]{:S(2)}, u32[]{:S(2)}) %collective-permute-start.10) | collective-permute-done | bytes 1572896 | tf_op jit(solution)/shard_map/ppermute | solution.py:23
  230.3 27.1 %collective-permute-done.44 = bf16[768,512]{1,0:T(8,128)(2,1)S(1)} collective-permute-done((bf16[768,512]{1,0:T(8,128)(2,1)S(1)}, bf16[768,512]{1,0:T(8,128)(2,1)S(1)}, u32[]{:S(2)}, u32[]{:S(2)}) %collective-permute-start.44) | collective-permute-done | bytes 786464 | tf_op jit(solution)/shard_map/ppermute | solution.py:23
  259.2 16.0 %collective-permute-done.11 = bf16[768,512]{1,0:T(8,128)(2,1)S(1)} collective-permute-done((bf16[768,512]{1,0:T(8,128)(2,1)S(1)}, bf16[768,512]{1,0:T(8,128)(2,1)S(1)}, u32[]{:S(2)}, u32[]{:S(2)}) %collective-permute-start.11) | collective-permute-done | bytes 786464 | tf_op jit(solution)/shard_map/ppermute | solution.py:23
  279.0 22.6 %collective-permute-done.45 = bf16[384,512]{1,0:T(8,128)(2,1)S(1)} collective-permute-done((bf16[384,512]{1,0:T(8,128)(2,1)S(1)}, bf16[384,512]{1,0:T(8,128)(2,1)S(1)}, u32[]{:S(2)}, u32[]{:S(2)}) %collective-permute-start.45) | collective-permute-done | bytes 393248 | tf_op jit(solution)/shard_map/ppermute | solution.py:23
  301.6 8.4 %collective-permute-done.12 = bf16[384,512]{1,0:T(8,128)(2,1)S(1)} collective-permute-done((bf16[384,512]{1,0:T(8,128)(2,1)S(1)}, bf16[384,512]{1,0:T(8,128)(2,1)S(1)}, u32[]{:S(2)}, u32[]{:S(2)}) %collective-permute-start.12) | collective-permute-done | bytes 393248 | tf_op jit(solution)/shard_map/ppermute | solution.py:23
  310.1 7.9 %fusion.152 = (bf16[384,512]{1,0:T(8,128)(2,1)S(1)}, bf16[384,512]{1,0:T(8,128)(2,1)S(1)}, bf16[384,512]{1,0:T(8,128)(2,1)S(1)}, bf16[384,512]{1,0:T(8,128)(2,1)S(1)}) fusion(bf16[384,512]{1,0:T(8,128)(2,1)S(1)} %collective-permute-done.61, bf16[768,512]{1,0:T(8,128)(2,1)S(1)} %add_convert_fusion.1, f32[384]{0:T(512)S(1)} %dynamic-slice_convert_fusion, ...), kind=kLoop, calls=%fused_computation.218 | loop fusion | flops 54263808 | bytes 4720128 | tf_op jit(solution)/shard_map/convert_element_type | solution.py:149
  323.5 14.6 %collective-permute-done.62 = bf16[384,512]{1,0:T(8,128)(2,1)S(1)} collective-permute-done((bf16[384,512]{1,0:T(8,128)(2,1)S(1)}, bf16[384,512]{1,0:T(8,128)(2,1)S(1)}, u32[]{:S(2)}, u32[]{:S(2)}) %collective-permute-start.62) | collective-permute-done | bytes 393248 | tf_op jit(solution)/shard_map/ppermute | solution.py:23
  343.7 11.3 %collective-permute-done.30 = bf16[384,512]{1,0:T(8,128)(2,1)S(1)} collective-permute-done((bf16[384,512]{1,0:T(8,128)(2,1)S(1)}, bf16[384,512]{1,0:T(8,128)(2,1)S(1)}, u32[]{:S(2)}, u32[]{:S(2)}) %collective-permute-start.30) | collective-permute-done | bytes 393248 | tf_op jit(solution)/shard_map/ppermute | solution.py:23
  359.3 10.2 %collective-permute-done.31 = bf16[384,512]{1,0:T(8,128)(2,1)S(1)} collective-permute-done((bf16[384,512]{1,0:T(8,128)(2,1)S(1)}, bf16[384,512]{1,0:T(8,128)(2,1)S(1)}, u32[]{:S(2)}, u32[]{:S(2)}) %collective-permute-start.31) | collective-permute-done | bytes 393248 | tf_op jit(solution)/shard_map/ppermute | solution.py:23
  372.2 16.3 %collective-permute-done.13 = bf16[384,512]{1,0:T(8,128)(2,1)S(1)} collective-permute-done((bf16[384,512]{1,0:T(8,128)(2,1)S(1)}, bf16[384,512]{1,0:T(8,128)(2,1)S(1)}, u32[]{:S(2)}, u32[]{:S(2)}) %collective-permute-start.13) | collective-permute-done | bytes 393248 | tf_op jit(solution)/shard_map/ppermute | solution.py:23
  394.4 12.1 %collective-permute-start.65 = (bf16[1536,256]{0,1:T(8,128)(2,1)S(1)}, bf16[1536,256]{0,1:T(8,128)(2,1)S(1)}, u32[]{:S(2)}, u32[]{:S(2)}) collective-permute-start(bf16[1536,256]{0,1:T(8,128)(2,1)S(1)} %slice.225), channel_id=1, source_target_pairs={{0,1},{1,0},{2,3},{3,2},{4,5},{5,4},{6,7},{7,6},{8,9},{9,8},{10,11... | collective-permute-start | bytes 2359304 | tf_op jit(solution)/shard_map/ppermute | solution.py:23
  406.5 4.7 collective-permute-done.48
  411.2 10.5 %collective-permute-start.33 = (bf16[1536,256]{0,1:T(8,128)(2,1)S(1)}, bf16[1536,256]{0,1:T(8,128)(2,1)S(1)}, u32[]{:S(2)}, u32[]{:S(2)}) collective-permute-start(bf16[1536,256]{0,1:T(8,128)(2,1)S(1)} %slice.205), channel_id=1, source_target_pairs={{0,1},{1,0},{2,3},{3,2},{4,5},{5,4},{6,7},{7,6},{8,9},{9,8},{10,11... | collective-permute-start | bytes 2359304 | tf_op jit(solution)/shard_map/ppermute | solution.py:23
  445.5 3.7 collective-permute-done.34
  449.2 8.4 %collective-permute-done.50 = bf16[1536,128]{0,1:T(8,128)(2,1)} collective-permute-done((bf16[1536,128]{0,1:T(8,128)(2,1)}, bf16[1536,128]{0,1:T(8,128)(2,1)}, u32[]{:S(2)}, u32[]{:S(2)}) %collective-permute-start.50) | collective-permute-done | bytes 393248 | tf_op jit(solution)/shard_map/ppermute | solution.py:23
  457.6 8.4 %collective-permute-done.17 = bf16[1536,128]{0,1:T(8,128)(2,1)} collective-permute-done((bf16[1536,128]{0,1:T(8,128)(2,1)}, bf16[1536,128]{0,1:T(8,128)(2,1)}, u32[]{:S(2)}, u32[]{:S(2)}) %collective-permute-start.17) | collective-permute-done | bytes 393248 | tf_op jit(solution)/shard_map/ppermute | solution.py:23
  473.5 4.9 collective-permute-start.20
  485.1 4.5 collective-permute-done.36
  500.2 3.7 collective-permute-done.70
  504.0 8.1 %fusion.8 = bf16[768,1280]{1,0:T(8,128)(2,1)} fusion(bf16[768,1280]{1,0:T(8,128)(2,1)S(1)} %copy-done.14, bf16[768,2560]{0,1:T(8,128)(2,1)S(1)} %constant_dynamic-update-slice_fusion.1, s32[2560]{0:T(1024)} %constant_dynamic-update-slice_fusion.15, pred[1280]{0:T(1024)(128)(4,1)S(1)} %fusion.1), kind=kOutput, calls=%fused_computation.33 | convolution fusion | flops 5038407680 | bytes 7875840 | tf_op jit(solution)/shard_map/dot_general | solution.py:192
  (247 shorter events, 161.6 us)
Async XLA Ops:
  22.5 32.9 %collective-permute-start.57 = (bf16[1600,128]{1,0:T(8,128)(2,1)S(1)}, bf16[1600,128]{1,0:T(8,128)(2,1)}, u32[]{:S(2)}, u32[]{:S(2)}) collective-permute-start(bf16[1600,128]{1,0:T(8,128)(2,1)S(1)} %get-tuple-element.49), channel_id=1, source_target_pairs={{0,1},{1,0},{2,3},{3,2},{4,5},{5,4},{6,7},{7,6},{8,9},{9,8},{10,11... | collective-permute-start | bytes 1228808 | tf_op jit(solution)/shard_map/ppermute | solution.py:23
  52.7 36.4 %collective-permute-start.53 = (bf16[1600,128]{1,0:T(8,128)(2,1)S(1)}, bf16[1600,128]{1,0:T(8,128)(2,1)S(1)}, u32[]{:S(2)}, u32[]{:S(2)}) collective-permute-start(bf16[1600,128]{1,0:T(8,128)(2,1)S(1)} %get-tuple-element.44), channel_id=1, source_target_pairs={{0,2},{1,3},{2,0},{3,1},{4,6},{5,7},{6,4},{7,5},{8,10},{9,11},{10,... | collective-permute-start | bytes 1228808 | tf_op jit(solution)/shard_map/ppermute | solution.py:23
  55.1 40.1 %collective-permute-start.54 = (bf16[1600,128]{1,0:T(8,128)(2,1)S(1)}, bf16[1600,128]{1,0:T(8,128)(2,1)S(1)}, u32[]{:S(2)}, u32[]{:S(2)}) collective-permute-start(bf16[1600,128]{1,0:T(8,128)(2,1)S(1)} %get-tuple-element.44), channel_id=1, source_target_pairs={{0,1},{1,0},{2,3},{3,2},{4,5},{5,4},{6,7},{7,6},{8,9},{9,8},{10,11... | collective-permute-start | bytes 1228808 | tf_op jit(solution)/shard_map/ppermute | solution.py:23
  85.6 36.0 %collective-permute-start.59 = (bf16[1536,512]{1,0:T(8,128)(2,1)S(1)}, bf16[1536,512]{1,0:T(8,128)(2,1)S(1)}, u32[]{:S(2)}, u32[]{:S(2)}) collective-permute-start(bf16[1536,512]{1,0:T(8,128)(2,1)S(1)} %convolution_convert_fusion.1), channel_id=1, source_target_pairs={{0,4},{4,0},{8,12},{12,8},{16,20},{20,16},{24,28},{28,24},{1,5},{5... | collective-permute-start | bytes 4718600 | tf_op jit(solution)/shard_map/ppermute | solution.py:23
  91.1 64.2 %collective-permute-start.27 = (bf16[1536,512]{1,0:T(8,128)(2,1)S(1)}, bf16[1536,512]{1,0:T(8,128)(2,1)S(1)}, u32[]{:S(2)}, u32[]{:S(2)}) collective-permute-start(bf16[1536,512]{1,0:T(8,128)(2,1)S(1)} %convolution_convert_fusion.5), channel_id=1, source_target_pairs={{0,4},{4,0},{8,12},{12,8},{16,20},{20,16},{24,28},{28,24},{1,5},{5... | collective-permute-start | bytes 4718600 | tf_op jit(solution)/shard_map/ppermute | solution.py:23
  95.2 30.4 %collective-permute-start.22 = (bf16[1600,128]{1,0:T(8,128)(2,1)S(1)}, bf16[1600,128]{1,0:T(8,128)(2,1)S(1)}, u32[]{:S(2)}, u32[]{:S(2)}) collective-permute-start(bf16[1600,128]{1,0:T(8,128)(2,1)S(1)} %get-tuple-element.46), channel_id=1, source_target_pairs={{0,1},{1,0},{2,3},{3,2},{4,5},{5,4},{6,7},{7,6},{8,9},{9,8},{10,11... | collective-permute-start | bytes 1228808 | tf_op jit(solution)/shard_map/ppermute | solution.py:23
  121.6 67.4 %collective-permute-start.43 = (bf16[1536,512]{1,0:T(8,128)(2,1)S(1)}, bf16[1536,512]{1,0:T(8,128)(2,1)S(1)}, u32[]{:S(2)}, u32[]{:S(2)}) collective-permute-start(bf16[1536,512]{1,0:T(8,128)(2,1)S(1)} %convolution_convert_fusion.3), channel_id=1, source_target_pairs={{0,4},{4,0},{8,12},{12,8},{16,20},{20,16},{24,28},{28,24},{1,5},{5... | collective-permute-start | bytes 4718600 | tf_op jit(solution)/shard_map/ppermute | solution.py:23
  125.6 33.4 %collective-permute-start.38 = (bf16[1600,128]{1,0:T(8,128)(2,1)S(1)}, bf16[1600,128]{1,0:T(8,128)(2,1)S(1)}, u32[]{:S(2)}, u32[]{:S(2)}) collective-permute-start(bf16[1600,128]{1,0:T(8,128)(2,1)S(1)} %get-tuple-element.48), channel_id=1, source_target_pairs={{0,1},{1,0},{2,3},{3,2},{4,5},{5,4},{6,7},{7,6},{8,9},{9,8},{10,11... | collective-permute-start | bytes 1228808 | tf_op jit(solution)/shard_map/ppermute | solution.py:23
  127.1 32.9 %collective-permute-start.4 = (bf16[1600,128]{1,0:T(8,128)(2,1)S(1)}, bf16[1600,128]{1,0:T(8,128)(2,1)S(1)}, u32[]{:S(2)}, u32[]{:S(2)}) collective-permute-start(bf16[1600,128]{1,0:T(8,128)(2,1)S(1)} %get-tuple-element.51), channel_id=1, source_target_pairs={{0,2},{1,3},{2,0},{3,1},{4,6},{5,7},{6,4},{7,5},{8,10},{9,11},{10,... | collective-permute-start | bytes 1228808 | tf_op jit(solution)/shard_map/ppermute | solution.py:23
  128.4 33.4 %collective-permute-start.39 = (bf16[1600,128]{1,0:T(8,128)(2,1)S(1)}, bf16[1600,128]{1,0:T(8,128)(2,1)S(1)}, u32[]{:S(2)}, u32[]{:S(2)}) collective-permute-start(bf16[1600,128]{1,0:T(8,128)(2,1)S(1)} %collective-permute-done.37), channel_id=1, source_target_pairs={{0,1},{1,0},{2,3},{3,2},{4,5},{5,4},{6,7},{7,6},{8,9},{9,8},{10,11... | collective-permute-start | bytes 1228808 | tf_op jit(solution)/shard_map/ppermute | solution.py:23
  155.3 67.4 %collective-permute-start.10 = (bf16[1536,512]{1,0:T(8,128)(2,1)S(1)}, bf16[1536,512]{1,0:T(8,128)(2,1)S(1)}, u32[]{:S(2)}, u32[]{:S(2)}) collective-permute-start(bf16[1536,512]{1,0:T(8,128)(2,1)S(1)} %convolution_convert_fusion.7), channel_id=1, source_target_pairs={{0,4},{4,0},{8,12},{12,8},{16,20},{20,16},{24,28},{28,24},{1,5},{5... | collective-permute-start | bytes 4718600 | tf_op jit(solution)/shard_map/ppermute | solution.py:23
  159.0 181.7 %collective-permute-start = (bf16[768,1536]{1,0:T(8,128)(2,1)S(1)}, bf16[768,1536]{1,0:T(8,128)(2,1)S(1)}, u32[]{:S(2)}, u32[]{:S(2)}) collective-permute-start(bf16[768,1536]{1,0:T(8,128)(2,1)S(1)} %copy-done.9), channel_id=1, source_target_pairs={{0,4},{4,0},{8,12},{12,8},{16,20},{20,16},{24,28},{28,24},{1,5},{5... | collective-permute-start | bytes 7077896 | tf_op jit(solution)/shard_map/ppermute | solution.py:23
  160.0 33.5 %collective-permute-start.5 = (bf16[1600,128]{1,0:T(8,128)(2,1)S(1)}, bf16[1600,128]{1,0:T(8,128)(2,1)S(1)}, u32[]{:S(2)}, u32[]{:S(2)}) collective-permute-start(bf16[1600,128]{1,0:T(8,128)(2,1)S(1)} %get-tuple-element.51), channel_id=1, source_target_pairs={{0,1},{1,0},{2,3},{3,2},{4,5},{5,4},{6,7},{7,6},{8,9},{9,8},{10,11... | collective-permute-start | bytes 1228808 | tf_op jit(solution)/shard_map/ppermute | solution.py:23
  161.8 32.0 %collective-permute-start.6 = (bf16[1600,128]{1,0:T(8,128)(2,1)S(1)}, bf16[1600,128]{1,0:T(8,128)(2,1)S(1)}, u32[]{:S(2)}, u32[]{:S(2)}) collective-permute-start(bf16[1600,128]{1,0:T(8,128)(2,1)S(1)} %collective-permute-done.4), channel_id=1, source_target_pairs={{0,1},{1,0},{2,3},{3,2},{4,5},{5,4},{6,7},{7,6},{8,9},{9,8},{10,11... | collective-permute-start | bytes 1228808 | tf_op jit(solution)/shard_map/ppermute | solution.py:23
  189.0 38.3 %collective-permute-start.60 = (bf16[768,512]{1,0:T(8,128)(2,1)S(1)}, bf16[768,512]{1,0:T(8,128)(2,1)S(1)}, u32[]{:S(2)}, u32[]{:S(2)}) collective-permute-start(bf16[768,512]{1,0:T(8,128)(2,1)S(1)} %slice.221), channel_id=1, source_target_pairs={{0,8},{4,12},{8,0},{12,4},{16,24},{20,28},{24,16},{28,20},{1,9},{5... | collective-permute-start | bytes 2359304 | tf_op jit(solution)/shard_map/ppermute | solution.py:23
  193.6 36.3 %collective-permute-start.28 = (bf16[768,512]{1,0:T(8,128)(2,1)S(1)}, bf16[768,512]{1,0:T(8,128)(2,1)S(1)}, u32[]{:S(2)}, u32[]{:S(2)}) collective-permute-start(bf16[768,512]{1,0:T(8,128)(2,1)S(1)} %slice.201), channel_id=1, source_target_pairs={{0,8},{4,12},{8,0},{12,4},{16,24},{20,28},{24,16},{28,20},{1,9},{5... | collective-permute-start | bytes 2359304 | tf_op jit(solution)/shard_map/ppermute | solution.py:23
  193.8 63.6 %collective-permute-start.44 = (bf16[768,512]{1,0:T(8,128)(2,1)S(1)}, bf16[768,512]{1,0:T(8,128)(2,1)S(1)}, u32[]{:S(2)}, u32[]{:S(2)}) collective-permute-start(bf16[768,512]{1,0:T(8,128)(2,1)S(1)} %slice.211), channel_id=1, source_target_pairs={{0,8},{4,12},{8,0},{12,4},{16,24},{20,28},{24,16},{28,20},{1,9},{5... | collective-permute-start | bytes 2359304 | tf_op jit(solution)/shard_map/ppermute | solution.py:23
  225.9 49.2 %collective-permute-start.11 = (bf16[768,512]{1,0:T(8,128)(2,1)S(1)}, bf16[768,512]{1,0:T(8,128)(2,1)S(1)}, u32[]{:S(2)}, u32[]{:S(2)}) collective-permute-start(bf16[768,512]{1,0:T(8,128)(2,1)S(1)} %slice.191), channel_id=1, source_target_pairs={{0,8},{4,12},{8,0},{12,4},{16,24},{20,28},{24,16},{28,20},{1,9},{5... | collective-permute-start | bytes 2359304 | tf_op jit(solution)/shard_map/ppermute | solution.py:23
  227.5 51.2 %collective-permute-start.61 = (bf16[384,512]{1,0:T(8,128)(2,1)S(1)}, bf16[384,512]{1,0:T(8,128)(2,1)S(1)}, u32[]{:S(2)}, u32[]{:S(2)}) collective-permute-start(bf16[384,512]{1,0:T(8,128)(2,1)S(1)} %slice.223), channel_id=1, source_target_pairs={{0,16},{4,20},{8,24},{12,28},{16,0},{20,4},{24,8},{28,12},{1,17},{... | collective-permute-start | bytes 1179656 | tf_op jit(solution)/shard_map/ppermute | solution.py:23
  230.2 48.9 %collective-permute-start.29 = (bf16[384,512]{1,0:T(8,128)(2,1)S(1)}, bf16[384,512]{1,0:T(8,128)(2,1)S(1)}, u32[]{:S(2)}, u32[]{:S(2)}) collective-permute-start(bf16[384,512]{1,0:T(8,128)(2,1)S(1)} %slice.203), channel_id=1, source_target_pairs={{0,16},{4,20},{8,24},{12,28},{16,0},{20,4},{24,8},{28,12},{1,17},{... | collective-permute-start | bytes 1179656 | tf_op jit(solution)/shard_map/ppermute | solution.py:23
  257.7 43.9 %collective-permute-start.45 = (bf16[384,512]{1,0:T(8,128)(2,1)S(1)}, bf16[384,512]{1,0:T(8,128)(2,1)S(1)}, u32[]{:S(2)}, u32[]{:S(2)}) collective-permute-start(bf16[384,512]{1,0:T(8,128)(2,1)S(1)} %slice.213), channel_id=1, source_target_pairs={{0,16},{4,20},{8,24},{12,28},{16,0},{20,4},{24,8},{28,12},{1,17},{... | collective-permute-start | bytes 1179656 | tf_op jit(solution)/shard_map/ppermute | solution.py:23
  275.4 34.6 %collective-permute-start.12 = (bf16[384,512]{1,0:T(8,128)(2,1)S(1)}, bf16[384,512]{1,0:T(8,128)(2,1)S(1)}, u32[]{:S(2)}, u32[]{:S(2)}) collective-permute-start(bf16[384,512]{1,0:T(8,128)(2,1)S(1)} %slice.193), channel_id=1, source_target_pairs={{0,16},{4,20},{8,24},{12,28},{16,0},{20,4},{24,8},{28,12},{1,17},{... | collective-permute-start | bytes 1179656 | tf_op jit(solution)/shard_map/ppermute | solution.py:23
  278.8 166.0 %collective-permute-start.18 = (bf16[768]{0:T(1024)(128)(2,1)}, bf16[768]{0:T(1024)(128)(2,1)}, u32[]{:S(2)}, u32[]{:S(2)}) collective-permute-start(bf16[768]{0:T(1024)(128)(2,1)} %param.15), channel_id=1, source_target_pairs={{0,4},{4,0},{8,12},{12,8},{16,20},{20,16},{24,28},{28,24},{1,5},{5... | collective-permute-start | bytes 4616 | tf_op jit(solution)/shard_map/ppermute | solution.py:23
  323.5 31.5 %collective-permute-start.30 = (bf16[384,512]{1,0:T(8,128)(2,1)S(1)}, bf16[384,512]{1,0:T(8,128)(2,1)S(1)}, u32[]{:S(2)}, u32[]{:S(2)}) collective-permute-start(bf16[384,512]{1,0:T(8,128)(2,1)S(1)} %get-tuple-element.75), channel_id=1, source_target_pairs={{0,16},{4,20},{8,24},{12,28},{16,0},{20,4},{24,8},{28,12},{1,17},{... | collective-permute-start | bytes 1179656 | tf_op jit(solution)/shard_map/ppermute | solution.py:23
  340.7 28.8 %collective-permute-start.31 = (bf16[384,512]{1,0:T(8,128)(2,1)S(1)}, bf16[384,512]{1,0:T(8,128)(2,1)S(1)}, u32[]{:S(2)}, u32[]{:S(2)}) collective-permute-start(bf16[384,512]{1,0:T(8,128)(2,1)S(1)} %get-tuple-element.75), channel_id=1, source_target_pairs={{0,8},{4,12},{8,0},{12,4},{16,24},{20,28},{24,16},{28,20},{1,9},{5... | collective-permute-start | bytes 1179656 | tf_op jit(solution)/shard_map/ppermute | solution.py:23
  342.2 27.3 %collective-permute-start.46 = (bf16[384,512]{1,0:T(8,128)(2,1)S(1)}, bf16[384,512]{1,0:T(8,128)(2,1)S(1)}, u32[]{:S(2)}, u32[]{:S(2)}) collective-permute-start(bf16[384,512]{1,0:T(8,128)(2,1)S(1)} %get-tuple-element.76), channel_id=1, source_target_pairs={{0,16},{4,20},{8,24},{12,28},{16,0},{20,4},{24,8},{28,12},{1,17},{... | collective-permute-start | bytes 1179656 | tf_op jit(solution)/shard_map/ppermute | solution.py:23
  355.0 33.6 %collective-permute-start.13 = (bf16[384,512]{1,0:T(8,128)(2,1)S(1)}, bf16[384,512]{1,0:T(8,128)(2,1)S(1)}, u32[]{:S(2)}, u32[]{:S(2)}) collective-permute-start(bf16[384,512]{1,0:T(8,128)(2,1)S(1)} %get-tuple-element.77), channel_id=1, source_target_pairs={{0,16},{4,20},{8,24},{12,28},{16,0},{20,4},{24,8},{28,12},{1,17},{... | collective-permute-start | bytes 1179656 | tf_op jit(solution)/shard_map/ppermute | solution.py:23
  355.0 33.6 %collective-permute-start.32 = (bf16[384,512]{1,0:T(8,128)(2,1)S(1)}, bf16[384,512]{1,0:T(8,128)(2,1)S(1)}, u32[]{:S(2)}, u32[]{:S(2)}) collective-permute-start(bf16[384,512]{1,0:T(8,128)(2,1)S(1)} %collective-permute-done.30), channel_id=1, source_target_pairs={{0,8},{4,12},{8,0},{12,4},{16,24},{20,28},{24,16},{28,20},{1,9},{5... | collective-permute-start | bytes 1179656 | tf_op jit(solution)/shard_map/ppermute | solution.py:23
  369.5 55.0 %collective-permute-start.14 = (bf16[384,512]{1,0:T(8,128)(2,1)S(1)}, bf16[384,512]{1,0:T(8,128)(2,1)S(1)}, u32[]{:S(2)}, u32[]{:S(2)}) collective-permute-start(bf16[384,512]{1,0:T(8,128)(2,1)S(1)} %get-tuple-element.77), channel_id=1, source_target_pairs={{0,8},{4,12},{8,0},{12,4},{16,24},{20,28},{24,16},{28,20},{1,9},{5... | collective-permute-start | bytes 1179656 | tf_op jit(solution)/shard_map/ppermute | solution.py:23
  388.6 36.0 %collective-permute-start.15 = (bf16[384,512]{1,0:T(8,128)(2,1)S(1)}, bf16[384,512]{1,0:T(8,128)(2,1)S(1)}, u32[]{:S(2)}, u32[]{:S(2)}) collective-permute-start(bf16[384,512]{1,0:T(8,128)(2,1)S(1)} %collective-permute-done.13), channel_id=1, source_target_pairs={{0,8},{4,12},{8,0},{12,4},{16,24},{20,28},{24,16},{28,20},{1,9},{5... | collective-permute-start | bytes 1179656 | tf_op jit(solution)/shard_map/ppermute | solution.py:23
  394.4 34.4 %collective-permute-start.65 = (bf16[1536,256]{0,1:T(8,128)(2,1)S(1)}, bf16[1536,256]{0,1:T(8,128)(2,1)S(1)}, u32[]{:S(2)}, u32[]{:S(2)}) collective-permute-start(bf16[1536,256]{0,1:T(8,128)(2,1)S(1)} %slice.225), channel_id=1, source_target_pairs={{0,1},{1,0},{2,3},{3,2},{4,5},{5,4},{6,7},{7,6},{8,9},{9,8},{10,11... | collective-permute-start | bytes 2359304 | tf_op jit(solution)/shard_map/ppermute | solution.py:23
  435.6 30.5 %collective-permute-start.17 = (bf16[1536,128]{0,1:T(8,128)(2,1)}, bf16[1536,128]{0,1:T(8,128)(2,1)}, u32[]{:S(2)}, u32[]{:S(2)}) collective-permute-start(bf16[1536,128]{0,1:T(8,128)(2,1)} %slice.197), channel_id=1, source_target_pairs={{0,2},{1,3},{2,0},{3,1},{4,6},{5,7},{6,4},{7,5},{8,10},{9,11},{10,... | collective-permute-start | bytes 1179656 | tf_op jit(solution)/shard_map/ppermute | solution.py:23
  (54 other events, 944.2 us)

commit v2 on v1

v2 whole, which is shorter than its diff:
```python
import functools

import jax
import jax.numpy as jnp
from jax import lax
from jax.experimental import pallas as pl
from jax.experimental.pallas import tpu as pltpu
from jax.sharding import PartitionSpec as P

D = 3200
TILE_SIDE = 32
TILE_ROWS = 256
HALF = 128
COLS = 512
F32 = jnp.float32
BF16 = jnp.bfloat16


def bit_reversed(bits):
    return [sum(((p >> b) & 1) << (bits - 1 - b) for b in range(bits)) for p in range(1 << bits)]


def swap(value, axis, mask):
    count = lax.axis_size(axis)
    return lax.ppermute(value, axis, [(i, i ^ mask) for i in range(count)])


def merge_kernel(patch_ref, order_ref, merged_ref, stats_ref):
    mixed = jnp.dot(patch_ref[...], order_ref[...], preferred_element_type=F32)
    total = jnp.zeros((1, HALF), F32)
    squares = jnp.zeros((1, HALF), F32)
    for slot in range(4):
        part = mixed[:, slot * HALF : (slot + 1) * HALF]
        merged_ref[0, slot] = part.astype(BF16)
        total += jnp.sum(part, axis=0, keepdims=True)
        squares += jnp.sum(part * part, axis=0, keepdims=True)
    stats_ref[0:1, :] = total
    stats_ref[1:2, :] = squares


def merge(patches):
    columns, width = patches.shape
    steps = width // COLS
    side = TILE_SIDE // 2
    source = lax.broadcasted_iota(jnp.int32, (COLS, COLS), 0)
    target = lax.broadcasted_iota(jnp.int32, (COLS, COLS), 1)
    slot = target // HALF
    row = target % HALF
    wanted = (
        (row // side) * (4 * side) + (slot // 2) * (2 * side) + (row % side) * 2 + slot % 2
    )
    order = (source == wanted).astype(BF16)
    return pl.pallas_call(
        merge_kernel,
        grid=(steps,),
        in_specs=[
            pl.BlockSpec((columns, COLS), lambda i: (0, i)),
            pl.BlockSpec((COLS, COLS), lambda i: (0, 0)),
        ],
        out_specs=[
            pl.BlockSpec((1, 4, columns, HALF), lambda i: (i, 0, 0, 0)),
            pl.BlockSpec((2, HALF), lambda i: (0, i)),
        ],
        out_shape=[
            jax.ShapeDtypeStruct((steps, 4, columns, HALF), BF16),
            jax.ShapeDtypeStruct((2, steps * HALF), F32),
        ],
        compiler_params=pltpu.CompilerParams(vmem_limit_bytes=32 * 1024 * 1024),
    )(patches, order)


def shards(
    patches,
    ln_gain,
    ln_bias,
    first_weight,
    first_bias,
    second_weight,
    second_bias,
    text_embeds,
    vis_pos,
):
    wide = lax.axis_size("wide")
    narrow = lax.axis_size("narrow")
    wide_bits = wide.bit_length() - 1
    narrow_bits = narrow.bit_length() - 1
    line = wide // 2
    wide_at = lax.axis_index("wide")
    narrow_at = lax.axis_index("narrow")
    side_at = wide_at % 2
    line_at = wide_at // 2
    columns = patches.shape[0]
    hidden = first_weight.shape[2]
    features = second_weight.shape[0]
    tiles = patches.shape[1] // (4 * TILE_ROWS)
    prompt_rows = text_embeds.shape[1]
    depth = 4 * columns
    block = hidden // line

    merged, stats = merge(patches)
    other_bias = swap(second_bias, "wide", 1)
    stats = stats + swap(stats, "wide", 1)
    stats, second_sent, other_bias = lax.optimization_barrier((stats, second_weight, other_bias))
    early = features // 3 // 16 * 16
    for bit in range(1, wide_bits):
        stats = stats + swap(stats, "wide", 1 << bit)
    entries = 4.0 * D
    row_mean = stats[0] / entries
    row_var = stats[1] / entries - row_mean * row_mean
    inverse = lax.rsqrt(row_var + 1e-05)
    gain = ln_gain.astype(F32)[:, :, None]
    shift = ln_bias.astype(F32)[:, :, None]

    def normed(half):
        values = lax.dynamic_index_in_dim(merged, half, 0, keepdims=False).astype(F32)
        mean = lax.dynamic_slice_in_dim(row_mean, half * HALF, HALF, 0)
        scale = lax.dynamic_slice_in_dim(inverse, half * HALF, HALF, 0)
        result = (values - mean[None, None, :]) * scale[None, None, :] * gain + shift
        return result.astype(BF16).reshape(depth, HALF)

    if line == 4:
        starts = [(line_at // 2 ^ i) * (hidden // 2) for i in range(2)]
    else:
        starts = [(line_at ^ i) * (hidden // line) for i in bit_reversed(wide_bits - 1)]
    block = hidden // len(starts)
    flat = first_weight.reshape(depth, hidden)
    own_bias = lax.dynamic_slice_in_dim(first_bias, starts[0], block, 0).astype(F32)[:, None]
    out_bias = jnp.concatenate([second_bias, other_bias]).astype(F32)[:, None]

    text_rows = narrow * prompt_rows - vis_pos.shape[0]
    first_row = narrow_at * prompt_rows
    grid = jnp.arange(prompt_rows, dtype=jnp.int32)[None, :]
    moves = {tile: [] for tile in range(tiles)}
    hits = {}
    for tile in range(tiles):
        spots = []
        for step in range(1 - narrow, narrow):
            pairs = []
            for source in range(narrow):
                target = source + step
                low = (source * tiles + tile) * TILE_ROWS
                if (
                    0 <= target < narrow
                    and low < (target + 1) * prompt_rows
                    and low + text_rows + TILE_ROWS > target * prompt_rows
                ):
                    pairs.append((source, target))
            if not pairs:
                continue
            moves[tile].append((step, pairs))
            whose = narrow_at - step
            at = (jnp.clip(whose, 0, narrow - 1) * tiles + tile) * TILE_ROWS
            spot = jnp.concatenate(
                [
                    lax.dynamic_slice_in_dim(vis_pos, at + half * HALF, HALF, 0) - first_row
                    for half in (side_at, 1 - side_at)
                ]
            )
            spots.append(jnp.where((whose >= 0) & (whose < narrow), spot, -1))
        hits[tile] = jnp.concatenate(spots)[:, None] == grid
    marked = functools.reduce(jnp.logical_or, [jnp.any(h, axis=0) for h in hits.values()])

    tile_order = bit_reversed(narrow_bits)
    outward = [(x, 2 + x) for x in (0, 1)] + [(6 + x, 4 + x) for x in (0, 1)]
    inward = [(b, a) for a, b in outward]
    middle = [(2 + x, 4 + x) for x in (0, 1)] + [(4 + x, 2 + x) for x in (0, 1)]
    is_middle = (line_at == 1) | (line_at == 2)
    have, joined = {}, set()

    def put(key, value, flying=False):
        have[key] = value
        joined.discard(key)
        if not flying:
            joined.add(key)

    def fly(key, value, axis, pairs):
        if isinstance(pairs, int):
            pairs = [(i, i ^ pairs) for i in range(lax.axis_size(axis))]
        put(key, lax.ppermute(value, axis, pairs), True)
        put(("sent", key), value)

    def sync(needs):
        joined.update(needs)
        keys = [k for k in have if k in joined]
        have.update(zip(keys, lax.optimization_barrier([have[k] for k in keys])))
        for key in keys:
            if key[0] == "sent":
                del have[key]

    def gather_step(key, tile, bits):
        if bits[0] == narrow_bits - 1:
            theirs, mine = normed_halves[tile]
            own = {"theirs": [theirs], "mine": [mine], "both": [theirs, mine]}[key]
            put((key, 0, tile), jnp.concatenate(own, axis=1))
        for bit in bits:
            for d in range(narrow):
                if d % (2 << bit) == 0:
                    fly((key, d + (1 << bit), tile), have[key, d, tile], "narrow", 1 << bit)

    def rows_of(key, tile):
        if (key, 0, tile) in have:
            return jnp.concatenate([have.pop((key, d, tile)) for d in tile_order], axis=1)
        at = 0 if key == "theirs" else HALF
        return jnp.concatenate(
            [have["both", d, tile][:, at : at + HALF] for d in tile_order], axis=1
        )

    def first_product(rows):
        return lax.dot_general(have["first",], rows, (((0,), (0,)), ((), ())), preferred_element_type=F32)

    def send_theirs(tile):
        sent = first_product(rows_of("theirs", tile)).astype(BF16)
        fly(("came", tile), sent, "wide", 1)

    def keep_mine(tile):
        put(("own", tile), first_product(rows_of("mine", tile)))
        for d in range(narrow):
            have.pop(("both", d, tile), None)

    def second_columns(at):
        parts = [second_weight, have["second", 0], have["second", 1]]
        return jnp.concatenate(
            [lax.dynamic_slice_in_dim(part, at, block, 1) for part in parts], axis=0
        )

    def far_out(tile):
        own, came = have.pop(("own", tile)), have.pop(("came", tile))
        far = (own[block:] + came[block:].astype(F32)).astype(BF16)
        put(("far", tile), far)
        fly(("far_came", tile), far, "wide", outward)
        near = (own[:block] + came[:block].astype(F32)).astype(BF16)
        put(("near", tile), near)
        fly(("near_came", tile), near, "wide", outward)

    def across(tile):
        far = have.pop(("far", tile)).astype(F32) + have.pop(("far_came", tile)).astype(F32)
        fly(("across", tile), far.astype(BF16), "wide", middle)

    def activate(tile):
        total = have.pop(("near", tile)).astype(F32) + have.pop(("near_came", tile)).astype(F32)
        total = total + have.pop(("across", tile)).astype(F32)
        act = jax.nn.gelu(total + own_bias, approximate=False).astype(BF16)
        put(("act", tile), act)
        fly(("far_act", tile), act, "wide", middle)
        fly(("near_act", tile), act, "wide", inward)

    def far_in(tile):
        fly(("far_act_end", tile), have["far_act", tile], "wide", inward)
        near = jnp.where(is_middle, have.pop(("act", tile)), have.pop(("near_act", tile)))
        put(("near_units", tile), near)

    def near_product(tile):
        near = have.pop(("near_units", tile))
        put(("value", tile), jnp.dot(second_columns(starts[0]), near, preferred_element_type=F32))

    def second_product(tile):
        if line == 4:
            far = have.pop(("far_act", tile)) + have.pop(("far_act_end", tile))
            more = jnp.dot(second_columns(starts[1]), far, preferred_element_type=F32)
            put(("value", tile), have["value", tile] + more)
        else:
            units = jnp.concatenate(have.pop(("acts", tile)), axis=0)
            second = jnp.concatenate([second_columns(s) for s in starts], axis=1)
            put(("value", tile), jnp.dot(second, units, preferred_element_type=F32))
        narrow_step(tile, 0)

    def halve(bit):
        def step(tile):
            if bit == 1:
                total = have.pop(("own", tile)) + have.pop(("came", tile)).astype(F32)
            else:
                total = have.pop(("sum", tile)).astype(F32) + have.pop(("part", tile)).astype(F32)
            total = total.astype(BF16)
            cut = total.shape[0] // 2
            put(("sum", tile), total[:cut])
            put(("part", tile), swap(total[cut:], "wide", 1 << bit))

        return step

    def double(bit):
        def step(tile):
            if bit == wide_bits - 1:
                total = have.pop(("sum", tile)).astype(F32) + have.pop(("part", tile)).astype(F32)
                act = jax.nn.gelu(total + own_bias, approximate=False).astype(BF16)
                put(("acts", tile), [act])
            acts = have["acts", tile]
            put(("acts", tile), acts + [swap(act, "wide", 1 << bit) for act in acts])

        return step

    def narrow_step(tile, bit):
        value = have["value", tile]
        if bit:
            value = value.astype(F32) + have["part", tile].astype(F32)
        value = value.astype(BF16)
        cut = value.shape[1] // 2
        fly(("part", tile), value[:, cut:], "narrow", 1 << bit)
        put(("value", tile), value[:, :cut])

    def trade(tile):
        value = have.pop(("value", tile)).astype(F32) + have.pop(("part", tile)).astype(F32)
        visual = (value + out_bias).astype(BF16)
        put(("kept", tile), visual[:features])
        fly(("traded", tile), visual[features:], "wide", 1)

    def halo(tile):
        whole = jnp.concatenate([have.pop(("kept", tile)), have.pop(("traded", tile))], axis=1)
        for step, pairs in moves[tile]:
            if step:
                fly(("moved", step, tile), whole, "narrow", pairs)
            else:
                put(("moved", step, tile), whole)

    def place(tile):
        moved = jnp.concatenate([have.pop(("moved", step, tile)) for step, _ in moves[tile]], axis=1)
        more = jnp.dot(moved, hits[tile].astype(BF16), preferred_element_type=F32)
        put(("placed",), have["placed",] + more.astype(BF16))

    def late_second():
        fly(("second", 1), have.pop(("second_late",))[early:], "wide", 1)

    def order_first():
        flat = have["first",]
        cut = [lax.dynamic_slice_in_dim(flat, s, block, 1) for s in starts]
        put(("first",), jnp.concatenate(cut, axis=1))

    def clear_marked():
        put(("placed",), jnp.where(marked[None, :], jnp.zeros((), BF16), have["placed",]))

    normed_halves = {
        tile: (normed(2 * tile + 1 - side_at), normed(2 * tile + side_at)) for tile in range(tiles)
    }
    high, low = [narrow_bits - 1], list(reversed(range(narrow_bits - 1)))
    put(("first",), flat)
    put(("placed",), text_embeds)
    put(("second_late",), second_sent)
    fly(("second", 0), second_sent[:early], "wide", 1)

    events = []

    def at(time, needs, step, *args):
        events.append((time, len(events), needs, step, args))

    def of(key, tile, bits):
        return [(key, d + (1 << b), tile) for b in bits for d in range(narrow) if d % (2 << b) == 0]

    at(20, [], gather_step, "theirs", 0, high)
    at(21, [], gather_step, "mine", 0, high)
    at(22, [], order_first)
    at(30, of("theirs", 0, high), gather_step, "theirs", 0, low)
    at(31, [], gather_step, "both", 1, high)
    at(34, of("theirs", 0, low) + [("second", 0)], send_theirs, 0)
    at(40, of("mine", 0, high), gather_step, "mine", 0, low)
    at(41, [], clear_marked)
    at(46, of("mine", 0, low), keep_mine, 0)
    at(60, of("both", 1, high), gather_step, "both", 1, low)
    at(61, [], gather_step, "both", 2, high)
    at(64, of("both", 1, low), send_theirs, 1)
    for tile in range(tiles):
        base = 82 + 38 * tile
        late = 82 + 38 * (tiles - 1) + 38
        if line == 4:
            at(base, [("came", tile)], far_out, tile)
            at(base + 21, [("far_came", tile)], across, tile)
            at(base + 44, [("across", tile), ("near_came", tile)], activate, tile)
            at(base + 67, [("far_act", tile), ("near_act", tile)], far_in, tile)
            at(max(base + 68, late + tile), [("second", 1)], near_product, tile)
            ready = max(base + 90, late + 2 + tile)
            at(ready, [("far_act_end", tile)], second_product, tile)
        else:
            for i, bit in enumerate(range(1, wide_bits)):
                at(base + 10 * i, [("part", tile)] if i else [("came", tile)], halve(bit), tile)
            for i, bit in enumerate(reversed(range(1, wide_bits))):
                needs = [] if i else [("part", tile)]
                at(base + 45 + 10 * i, needs, double(bit), tile)
            ready = max(base + 90, late + 2 + tile)
            at(ready, [("second", 1)], second_product, tile)
        for bit in range(1, narrow_bits):
            at(ready + 4 * bit, [("part", tile)], narrow_step, tile, bit)
        after = ready + 4 * narrow_bits + 9
        at(after, [("part", tile)], trade, tile)
        at(after + 8, [("traded", tile)], halo, tile)
        flown = [("moved", step, tile) for step, _ in moves[tile] if step]
        at(after + 16, flown, place, tile)
        if tile + 1 < tiles:
            at(base + 32, [], keep_mine, tile + 1)
        if tile + 2 < tiles:
            at(base + 9, of("both", tile + 2, high), gather_step, "both", tile + 2, low)
            at(base + 14, of("both", tile + 2, low), send_theirs, tile + 2)
        if tile + 3 < tiles:
            at(base + 10, [], gather_step, "both", tile + 3, high)
    at(82 + 38 * (tiles - 3) + 15, [], late_second)
    for _, _, needs, step, args in sorted(events, key=lambda e: e[:2]):
        sync(needs)
        step(*args)
    return have["placed",]


def solution(mesh):
    in_specs = (
        P("wide", "narrow"),
        P(None, "wide"),
        P(None, "wide"),
        P(None, "wide", "narrow"),
        P("narrow"),
        P("wide", "narrow"),
        P("wide"),
        P("wide", "narrow"),
        P(),
    )
    out_specs = P("wide", "narrow")
    return jax.shard_map(shards, mesh=mesh, in_specs=in_specs, out_specs=out_specs, check_vma=False)
```

time: 518 us -> 405 us (0.78)
  waiting for transfers between devices: 292 us -> 165 us
  starting transfers between devices: 101 us -> 122 us
  local copies, waits for them, and re-layouts: 33.6 us -> 20.6 us
    ppermute x65 -> x4, waiting for transfers between devices: 283 us -> 0.63 us  [swap(): return lax.ppermute(value, axis, [(i, i ^ mask) for i in range(count)])]
    ppermute x6 -> x63, waiting for transfers between devices: 9.29 us -> 164 us  [fly(): put(key, lax.ppermute(value, axis, pairs), True)]
    ppermute x6 -> x63, starting transfers between devices: 12.6 us -> 116 us  [fly(): put(key, lax.ppermute(value, axis, pairs), True)]
    ppermute x65 -> x4, starting transfers between devices: 88.2 us -> 6.19 us  [swap(): return lax.ppermute(value, axis, [(i, i ^ mask) for i in range(count)])]
    gather x10 -> x0, local copies, waits for them, and re-layouts: 20.7 us -> none  [shards(): lax.dynamic_slice_in_dim(vis_pos, at, TILE_ROWS, 0)[in_tile] - first_row]
    convert_element_type x11 -> x25, other arithmetic: 12.2 us -> 28.7 us  [the longest x4 17.9 us: activate(): act = jax.nn.gelu(total + own_bias, approximate=False).astype(BF16)]
    unnamed x10 -> x1, other arithmetic: 11.6 us -> 0.01 us
    slice x20 -> x40, local copies, waits for them, and re-layouts: 3.74 us -> 11.8 us  [the longest x26 9.8 us: rows_of(): have['both', d, tile][:, at:at + HALF]]
  transfers between devices with their start and end apart: 71 -> 67, of which waited for: 28 -> 29; matrix products, arithmetic and copies ran while one was open for 20% -> 23% of each run, Pallas kernels for 0% -> 0%
where the time goes in v2:
time: 405 us; the launch traced here: 399 us
  waiting for transfers between devices  165 us (41%)
  starting transfers between devices  122 us (30%)
  matrix products  46.8 us (12%)
  other arithmetic  38.8 us (10%)
  local copies, waits for them, and re-layouts  20.6 us (5%)
    ppermute x63, waiting for transfers between devices, fly(): put(key, lax.ppermute(value, axis, pairs), True)  164 us
    ppermute x63, starting transfers between devices, fly(): put(key, lax.ppermute(value, axis, pairs), True)  116 us
    dot_general x8, matrix products, first_product(): lax.dot_general(have['first',], rows, (((0,), (0,)), ((), ())), preferred...  29.2 us
    convert_element_type x4, other arithmetic, activate(): act = jax.nn.gelu(total + own_bias, approximate=False).astype(BF16)  17.9 us
    slice x26, local copies, waits for them, and re-layouts, rows_of(): have['both', d, tile][:, at:at + HALF]  9.8 us
  transfers between devices with their start and end apart: 67, of which 29 were waited for; matrix products, arithmetic and copies ran while one was open for 23% of the time, Pallas kernels for 0%

profile of v2, /device:TPU:1, one launch (start us, length us, event | category | flops | bytes accessed | tf_op | source)
XLA Modules:
  0.0 398.9 jit_solution(18315566210581520416)
XLA Ops:
  2.1 3.4 shard_map.91
  28.2 3.9 collective-permute-start.6
  37.7 5.1 %collective-permute-done.8 = bf16[1600,128]{1,0:T(8,128)(2,1)S(1)} collective-permute-done((bf16[1600,128]{1,0:T(8,128)(2,1)S(1)}, bf16[1600,128]{1,0:T(8,128)(2,1)S(1)}, u32[]{:S(2)}, u32[]{:S(2)}) %collective-permute-start.8) | collective-permute-done | bytes 409632 | tf_op jit(solution)/shard_map/ppermute | solution.py:179
  50.0 10.4 %collective-permute-done.11 = bf16[1600,256]{1,0:T(8,128)(2,1)S(1)} collective-permute-done((bf16[1600,256]{1,0:T(8,128)(2,1)S(1)}, bf16[1600,256]{1,0:T(8,128)(2,1)S(1)}, u32[]{:S(2)}, u32[]{:S(2)}) %collective-permute-start.11) | collective-permute-done | bytes 819232 | tf_op jit(solution)/shard_map/ppermute | solution.py:179
  68.0 29.1 %collective-permute-done.14 = bf16[1536,512]{1,0:T(8,128)(2,1)S(1)} collective-permute-done((bf16[1536,512]{1,0:T(8,128)(2,1)S(1)}, bf16[1536,512]{1,0:T(8,128)(2,1)S(1)}, u32[]{:S(2)}, u32[]{:S(2)}) %collective-permute-start.14) | collective-permute-done | bytes 1572896 | tf_op jit(solution)/shard_map/ppermute | solution.py:179
  107.3 5.0 %convolution_convert_fusion.3 = bf16[1536,512]{1,0:T(8,128)(2,1)} fusion(bf16[1600,1536]{1,0:T(8,128)(2,1)S(1)} %pad_maximum_fusion, bf16[1600,128]{1,0:T(8,128)(2,1)S(1)} %slice.218, bf16[1600,128]{1,0:T(8,128)(2,1)S(1)} %slice.217, bf16[1600,128]{1,0:T(8,128)(2,1)S(1)} %slice.216, bf16[1600,128]{1,0:T(8,128)(2,1)S(1)} %slice.215), kind=kOutput, calls=%fused_computation.24 | convolution fusion | flops 2523922432 | bytes 8126464 | tf_op jit(solution)/shard_map/dot_general | solution.py:209
  112.3 6.6 %collective-permute-done.18 = bf16[768,512]{1,0:T(8,128)(2,1)S(1)} collective-permute-done((bf16[768,512]{1,0:T(8,128)(2,1)S(1)}, bf16[768,512]{1,0:T(8,128)(2,1)S(1)}, u32[]{:S(2)}, u32[]{:S(2)}) %collective-permute-start.18) | collective-permute-done | bytes 786464 | tf_op jit(solution)/shard_map/ppermute | solution.py:179
  123.1 16.5 %collective-permute-done.19 = bf16[1536,512]{1,0:T(8,128)(2,1)S(1)} collective-permute-done((bf16[1536,512]{1,0:T(8,128)(2,1)S(1)}, bf16[1536,512]{1,0:T(8,128)(2,1)S(1)}, u32[]{:S(2)}, u32[]{:S(2)}) %collective-permute-start.19) | collective-permute-done | bytes 1572896 | tf_op jit(solution)/shard_map/ppermute | solution.py:179
  141.1 4.9 %fusion.112 = bf16[768,512]{1,0:T(8,128)(2,1)} fusion(bf16[768,512]{1,0:T(8,128)(2,1)S(1)} %collective-permute-done.21, bf16[768,512]{1,0:T(8,128)(2,1)S(1)} %collective-permute-done.20, bf16[768,512]{1,0:T(8,128)(2,1)S(1)} %get-tuple-element.795, f32[768]{0:T(1024)S(1)} %dynamic-slice_convert_fusion), kind=kLoop, calls=%fused_computation.140 | loop fusion | flops 27918336 | bytes 3148800 | tf_op jit(solution)/shard_map/convert_element_type | solution.py:242
  158.9 5.7 %convolution_convert_fusion.2 = bf16[1536,512]{1,0:T(8,128)(2,1)S(1)} fusion(bf16[1600,1536]{1,0:T(8,128)(2,1)} %copy-done.2, bf16[1600,128]{1,0:T(8,128)(2,1)S(1)} %slice.230, bf16[1600,128]{1,0:T(8,128)(2,1)S(1)} %slice.229, bf16[1600,128]{1,0:T(8,128)(2,1)S(1)} %slice.228, bf16[1600,128]{1,0:T(8,128)(2,1)S(1)} %slice.227), kind=kOutput, calls=%fused_computation.23 | convolution fusion | flops 2523922432 | bytes 8126464 | tf_op jit(solution)/shard_map/dot_general | solution.py:209
  169.4 4.0 collective-permute-done.27
  177.7 8.6 %collective-permute-done.28 = bf16[1536,512]{1,0:T(8,128)(2,1)S(1)} collective-permute-done((bf16[1536,512]{1,0:T(8,128)(2,1)}, bf16[1536,512]{1,0:T(8,128)(2,1)S(1)}, u32[]{:S(2)}, u32[]{:S(2)}) %collective-permute-start.28) | collective-permute-done | bytes 1572896 | tf_op jit(solution)/shard_map/ppermute | solution.py:179
  188.4 4.2 %fusion.115 = bf16[768,512]{1,0:T(8,128)(2,1)S(1)} fusion(bf16[768,512]{1,0:T(8,128)(2,1)S(1)} %collective-permute-done.30, bf16[768,512]{1,0:T(8,128)(2,1)S(1)} %collective-permute-done.29, bf16[768,512]{1,0:T(8,128)(2,1)S(1)} %get-tuple-element.908, f32[768]{0:T(1024)S(1)} %dynamic-slice_convert_fusion), kind=kLoop, calls=%fused_computation.143 | loop fusion | flops 27918336 | bytes 3148800 | tf_op jit(solution)/shard_map/convert_element_type | solution.py:242
  194.9 4.3 %collective-permute-start.35 = (bf16[768,512]{1,0:T(8,128)(2,1)S(1)}, bf16[768,512]{1,0:T(8,128)(2,1)S(1)}, u32[]{:S(2)}, u32[]{:S(2)}) collective-permute-start(bf16[768,512]{1,0:T(8,128)(2,1)S(1)} %get-tuple-element.968), channel_id=1, source_target_pairs={{0,8},{4,12},{24,16},{28,20},{1,9},{5,13},{25,17},{29,21},{2,10},{... | collective-permute-start | bytes 2359304 | tf_op jit(solution)/shard_map/ppermute | solution.py:179
  199.2 4.5 %collective-permute-done.31 = bf16[768,512]{1,0:T(8,128)(2,1)S(1)} collective-permute-done((bf16[768,512]{1,0:T(8,128)(2,1)S(1)}, bf16[768,512]{1,0:T(8,128)(2,1)S(1)}, u32[]{:S(2)}, u32[]{:S(2)}) %collective-permute-start.31) | collective-permute-done | bytes 786464 | tf_op jit(solution)/shard_map/ppermute | solution.py:179
  204.9 6.1 %collective-permute-done.33 = bf16[768,512]{1,0:T(8,128)(2,1)S(1)} collective-permute-done((bf16[768,512]{1,0:T(8,128)(2,1)S(1)}, bf16[768,512]{1,0:T(8,128)(2,1)S(1)}, u32[]{:S(2)}, u32[]{:S(2)}) %collective-permute-start.33) | collective-permute-done | bytes 786464 | tf_op jit(solution)/shard_map/ppermute | solution.py:179
  218.4 10.5 %collective-permute-done.34 = bf16[1536,512]{1,0:T(8,128)(2,1)S(1)} collective-permute-done((bf16[1536,512]{1,0:T(8,128)(2,1)S(1)}, bf16[1536,512]{1,0:T(8,128)(2,1)S(1)}, u32[]{:S(2)}, u32[]{:S(2)}) %collective-permute-start.34) | collective-permute-done | bytes 1572896 | tf_op jit(solution)/shard_map/ppermute | solution.py:179
  231.8 4.2 %fusion.118 = bf16[768,512]{1,0:T(8,128)(2,1)S(1)} fusion(bf16[768,512]{1,0:T(8,128)(2,1)S(1)} %collective-permute-done.36, bf16[768,512]{1,0:T(8,128)(2,1)S(1)} %collective-permute-done.35, bf16[768,512]{1,0:T(8,128)(2,1)S(1)} %get-tuple-element.968, f32[768]{0:T(1024)S(1)} %dynamic-slice_convert_fusion), kind=kLoop, calls=%fused_computation.146 | loop fusion | flops 27918336 | bytes 3148800 | tf_op jit(solution)/shard_map/convert_element_type | solution.py:242
  242.1 8.2 %collective-permute-start.44 = (bf16[768,512]{1,0:T(8,128)(2,1)S(1)}, bf16[768,512]{1,0:T(8,128)(2,1)S(1)}, u32[]{:S(2)}, u32[]{:S(2)}) collective-permute-start(bf16[768,512]{1,0:T(8,128)(2,1)S(1)} %get-tuple-element.1066), channel_id=1, source_target_pairs={{0,8},{4,12},{24,16},{28,20},{1,9},{5,13},{25,17},{29,21},{2,10},{... | collective-permute-start | bytes 2359304 | tf_op jit(solution)/shard_map/ppermute | solution.py:179
  251.3 11.3 %collective-permute-done.40 = bf16[512,1536]{1,0:T(8,128)(2,1)S(1)} collective-permute-done((bf16[512,1536]{1,0:T(8,128)(2,1)S(1)}, bf16[512,1536]{1,0:T(8,128)(2,1)S(1)}, u32[]{:S(2)}, u32[]{:S(2)}) %collective-permute-start.40) | collective-permute-done | bytes 1572896 | tf_op jit(solution)/shard_map/ppermute | solution.py:179
  269.4 17.8 %collective-permute-start.43 = (bf16[1536,256]{1,0:T(8,128)(2,1)S(1)}, bf16[1536,256]{1,0:T(8,128)(2,1)S(1)}, u32[]{:S(2)}, u32[]{:S(2)}) collective-permute-start(bf16[1536,256]{1,0:T(8,128)(2,1)S(1)} %get-tuple-element.1235), channel_id=1, source_target_pairs={{0,1},{1,0},{2,3},{3,2},{4,5},{5,4},{6,7},{7,6},{8,9},{9,8},{10,11... | collective-permute-start | bytes 2359304 | tf_op jit(solution)/shard_map/ppermute | solution.py:179
  291.2 12.0 %collective-permute-start.46 = (bf16[1536,256]{1,0:T(8,128)(2,1)S(1)}, bf16[1536,256]{1,0:T(8,128)(2,1)S(1)}, u32[]{:S(2)}, u32[]{:S(2)}) collective-permute-start(bf16[1536,256]{1,0:T(8,128)(2,1)S(1)} %get-tuple-element.1233), channel_id=1, source_target_pairs={{0,1},{1,0},{2,3},{3,2},{4,5},{5,4},{6,7},{7,6},{8,9},{9,8},{10,11... | collective-permute-start | bytes 2359304 | tf_op jit(solution)/shard_map/ppermute | solution.py:179
  303.5 4.6 %fusion.121 = bf16[768,512]{1,0:T(8,128)(2,1)S(1)} fusion(bf16[768,512]{1,0:T(8,128)(2,1)S(1)} %collective-permute-done.45, bf16[768,512]{1,0:T(8,128)(2,1)S(1)} %collective-permute-done.44, bf16[768,512]{1,0:T(8,128)(2,1)S(1)} %get-tuple-element.1066, f32[768]{0:T(1024)S(1)} %dynamic-slice_convert_fusion), kind=kLoop, calls=%fused_computation.149 | loop fusion | flops 27918336 | bytes 3148800 | tf_op jit(solution)/shard_map/convert_element_type | solution.py:242
  316.8 5.2 %collective-permute-done.49 = bf16[1536,128]{1,0:T(8,128)(2,1)S(1)} collective-permute-done((bf16[1536,128]{1,0:T(8,128)(2,1)S(1)}, bf16[1536,128]{1,0:T(8,128)(2,1)S(1)}, u32[]{:S(2)}, u32[]{:S(2)}) %collective-permute-start.49) | collective-permute-done | bytes 393248 | tf_op jit(solution)/shard_map/ppermute | solution.py:179
  322.8 7.7 %collective-permute-done.50 = bf16[1536,128]{1,0:T(8,128)(2,1)S(1)} collective-permute-done((bf16[1536,128]{1,0:T(8,128)(2,1)S(1)}, bf16[1536,128]{1,0:T(8,128)(2,1)S(1)}, u32[]{:S(2)}, u32[]{:S(2)}) %collective-permute-start.50) | collective-permute-done | bytes 393248 | tf_op jit(solution)/shard_map/ppermute | solution.py:179
  331.3 4.3 %collective-permute-start.56 = (bf16[768,256]{1,0:T(8,128)(2,1)S(1)}, bf16[768,256]{1,0:T(8,128)(2,1)S(1)}, u32[]{:S(2)}, u32[]{:S(2)}) collective-permute-start(bf16[768,256]{1,0:T(8,128)(2,1)S(1)} %constant_dynamic-update-slice_fusion), channel_id=1, source_target_pairs={{1,0},{2,1},{3,2},{5,4},{6,5},{7,6},{9,8},{10,9},{11,10},{13,12},{... | collective-permute-start | bytes 1179656 | tf_op jit(solution)/shard_map/ppermute | solution.py:179
  351.3 5.2 %collective-permute-start.61 = (bf16[768,256]{1,0:T(8,128)(2,1)S(1)}, bf16[768,256]{1,0:T(8,128)(2,1)S(1)}, u32[]{:S(2)}, u32[]{:S(2)}) collective-permute-start(bf16[768,256]{1,0:T(8,128)(2,1)S(1)} %constant_dynamic-update-slice_fusion.4), channel_id=1, source_target_pairs={{0,1},{1,2},{4,5},{5,6},{8,9},{9,10},{12,13},{13,14},{16,17},{17,1... | collective-permute-start | bytes 1179656 | tf_op jit(solution)/shard_map/ppermute | solution.py:179
  356.5 4.5 %collective-permute-done.61 = bf16[768,256]{1,0:T(8,128)(2,1)S(1)} collective-permute-done((bf16[768,256]{1,0:T(8,128)(2,1)S(1)}, bf16[768,256]{1,0:T(8,128)(2,1)S(1)}, u32[]{:S(2)}, u32[]{:S(2)}) %collective-permute-start.61) | collective-permute-done | bytes 393248 | tf_op jit(solution)/shard_map/ppermute | solution.py:179
  370.9 9.2 %collective-permute-done.64 = bf16[1536,128]{1,0:T(8,128)(2,1)S(1)} collective-permute-done((bf16[1536,128]{1,0:T(8,128)(2,1)S(1)}, bf16[1536,128]{1,0:T(8,128)(2,1)S(1)}, u32[]{:S(2)}, u32[]{:S(2)}) %collective-permute-start.64) | collective-permute-done | bytes 393248 | tf_op jit(solution)/shard_map/ppermute | solution.py:179
  380.9 5.1 %collective-permute-done.65 = bf16[768,128]{1,0:T(8,128)(2,1)S(1)} collective-permute-done((bf16[768,128]{1,0:T(8,128)(2,1)S(1)}, bf16[768,128]{1,0:T(8,128)(2,1)S(1)}, u32[]{:S(2)}, u32[]{:S(2)}) %collective-permute-start.65) | collective-permute-done | bytes 196640 | tf_op jit(solution)/shard_map/ppermute | solution.py:179
  386.1 4.7 %collective-permute-start.66 = (bf16[768,256]{1,0:T(8,128)(2,1)S(1)}, bf16[768,256]{1,0:T(8,128)(2,1)S(1)}, u32[]{:S(2)}, u32[]{:S(2)}) collective-permute-start(bf16[768,256]{1,0:T(8,128)(2,1)S(1)} %constant_dynamic-update-slice_fusion.6), channel_id=1, source_target_pairs={{0,1},{1,2},{2,3},{4,5},{5,6},{6,7},{8,9},{9,10},{10,11},{12,13},{... | collective-permute-start | bytes 1179656 | tf_op jit(solution)/shard_map/ppermute | solution.py:179
  390.8 4.7 %collective-permute-done.66 = bf16[768,256]{1,0:T(8,128)(2,1)S(1)} collective-permute-done((bf16[768,256]{1,0:T(8,128)(2,1)S(1)}, bf16[768,256]{1,0:T(8,128)(2,1)S(1)}, u32[]{:S(2)}, u32[]{:S(2)}) %collective-permute-start.66) | collective-permute-done | bytes 393248 | tf_op jit(solution)/shard_map/ppermute | solution.py:179
  (327 shorter events, 155.4 us)
Async XLA Ops:
  33.5 26.8 %collective-permute-start.11 = (bf16[1600,256]{1,0:T(8,128)(2,1)S(1)}, bf16[1600,256]{1,0:T(8,128)(2,1)S(1)}, u32[]{:S(2)}, u32[]{:S(2)}) collective-permute-start(bf16[1600,256]{1,0:T(8,128)(2,1)S(1)} %pad_maximum_fusion.9), channel_id=1, source_target_pairs={{0,2},{1,3},{2,0},{3,1},{4,6},{5,7},{6,4},{7,5},{8,10},{9,11},{10,... | collective-permute-start | bytes 2457608 | tf_op jit(solution)/shard_map/ppermute | solution.py:179
  61.6 35.4 %collective-permute-start.14 = (bf16[1536,512]{1,0:T(8,128)(2,1)S(1)}, bf16[1536,512]{1,0:T(8,128)(2,1)S(1)}, u32[]{:S(2)}, u32[]{:S(2)}) collective-permute-start(bf16[1536,512]{1,0:T(8,128)(2,1)S(1)} %convolution_convert_fusion.5), channel_id=1, source_target_pairs={{0,4},{4,0},{8,12},{12,8},{16,20},{20,16},{24,28},{28,24},{1,5},{5... | collective-permute-start | bytes 4718600 | tf_op jit(solution)/shard_map/ppermute | solution.py:179
  62.0 35.7 %collective-permute-start.15 = (bf16[1600,256]{1,0:T(8,128)(2,1)S(1)}, bf16[1600,256]{1,0:T(8,128)(2,1)S(1)}, u32[]{:S(2)}, u32[]{:S(2)}) collective-permute-start(bf16[1600,256]{1,0:T(8,128)(2,1)S(1)} %pad_maximum_fusion.10), channel_id=1, source_target_pairs={{0,2},{1,3},{2,0},{3,1},{4,6},{5,7},{6,4},{7,5},{8,10},{9,11},{10,... | collective-permute-start | bytes 2457608 | tf_op jit(solution)/shard_map/ppermute | solution.py:179
  99.3 19.7 %collective-permute-start.18 = (bf16[768,512]{1,0:T(8,128)(2,1)S(1)}, bf16[768,512]{1,0:T(8,128)(2,1)S(1)}, u32[]{:S(2)}, u32[]{:S(2)}) collective-permute-start(bf16[768,512]{1,0:T(8,128)(2,1)S(1)} %get-tuple-element.756), channel_id=1, source_target_pairs={{0,8},{4,12},{24,16},{28,20},{1,9},{5,13},{25,17},{29,21},{2,10},{... | collective-permute-start | bytes 2359304 | tf_op jit(solution)/shard_map/ppermute | solution.py:179
  103.5 42.5 %collective-permute-start.22 = (bf16[1600,256]{1,0:T(8,128)(2,1)}, bf16[1600,256]{1,0:T(8,128)(2,1)}, u32[]{:S(2)}, u32[]{:S(2)}) collective-permute-start(bf16[1600,256]{1,0:T(8,128)(2,1)} %pad_maximum_fusion.11), channel_id=1, source_target_pairs={{0,2},{1,3},{2,0},{3,1},{4,6},{5,7},{6,4},{7,5},{8,10},{9,11},{10,... | collective-permute-start | bytes 2457608 | tf_op jit(solution)/shard_map/ppermute | solution.py:179
  104.7 34.9 %collective-permute-start.19 = (bf16[1536,512]{1,0:T(8,128)(2,1)S(1)}, bf16[1536,512]{1,0:T(8,128)(2,1)S(1)}, u32[]{:S(2)}, u32[]{:S(2)}) collective-permute-start(bf16[1536,512]{1,0:T(8,128)(2,1)S(1)} %convolution_convert_fusion.4), channel_id=1, source_target_pairs={{0,4},{4,0},{8,12},{12,8},{16,20},{20,16},{24,28},{28,24},{1,5},{5... | collective-permute-start | bytes 4718600 | tf_op jit(solution)/shard_map/ppermute | solution.py:179
  105.0 36.1 %collective-permute-start.20 = (bf16[768,512]{1,0:T(8,128)(2,1)S(1)}, bf16[768,512]{1,0:T(8,128)(2,1)S(1)}, u32[]{:S(2)}, u32[]{:S(2)}) collective-permute-start(bf16[768,512]{1,0:T(8,128)(2,1)S(1)} %get-tuple-element.795), channel_id=1, source_target_pairs={{0,8},{4,12},{24,16},{28,20},{1,9},{5,13},{25,17},{29,21},{2,10},{... | collective-permute-start | bytes 2359304 | tf_op jit(solution)/shard_map/ppermute | solution.py:179
  119.2 22.0 %collective-permute-start.21 = (bf16[768,512]{1,0:T(8,128)(2,1)S(1)}, bf16[768,512]{1,0:T(8,128)(2,1)S(1)}, u32[]{:S(2)}, u32[]{:S(2)}) collective-permute-start(bf16[768,512]{1,0:T(8,128)(2,1)S(1)} %add_convert_fusion.17), channel_id=1, source_target_pairs={{8,16},{12,20},{16,8},{20,12},{9,17},{13,21},{17,9},{21,13},{10,18... | collective-permute-start | bytes 2359304 | tf_op jit(solution)/shard_map/ppermute | solution.py:179
  147.9 18.9 %collective-permute-start.25 = (bf16[768,512]{1,0:T(8,128)(2,1)}, bf16[768,512]{1,0:T(8,128)(2,1)}, u32[]{:S(2)}, u32[]{:S(2)}) collective-permute-start(bf16[768,512]{1,0:T(8,128)(2,1)} %get-tuple-element.854), channel_id=1, source_target_pairs={{0,8},{4,12},{24,16},{28,20},{1,9},{5,13},{25,17},{29,21},{2,10},{... | collective-permute-start | bytes 2359304 | tf_op jit(solution)/shard_map/ppermute | solution.py:179
  151.0 35.3 %collective-permute-start.28 = (bf16[1536,512]{1,0:T(8,128)(2,1)}, bf16[1536,512]{1,0:T(8,128)(2,1)S(1)}, u32[]{:S(2)}, u32[]{:S(2)}) collective-permute-start(bf16[1536,512]{1,0:T(8,128)(2,1)} %convolution_convert_fusion.3), channel_id=1, source_target_pairs={{0,4},{4,0},{8,12},{12,8},{16,20},{20,16},{24,28},{28,24},{1,5},{5... | collective-permute-start | bytes 4718600 | tf_op jit(solution)/shard_map/ppermute | solution.py:179
  151.3 37.1 %collective-permute-start.29 = (bf16[768,512]{1,0:T(8,128)(2,1)S(1)}, bf16[768,512]{1,0:T(8,128)(2,1)S(1)}, u32[]{:S(2)}, u32[]{:S(2)}) collective-permute-start(bf16[768,512]{1,0:T(8,128)(2,1)S(1)} %get-tuple-element.908), channel_id=1, source_target_pairs={{0,8},{4,12},{24,16},{28,20},{1,9},{5,13},{25,17},{29,21},{2,10},{... | collective-permute-start | bytes 2359304 | tf_op jit(solution)/shard_map/ppermute | solution.py:179
  152.6 16.8 %collective-permute-start.26 = (bf16[768,512]{1,0:T(8,128)(2,1)}, bf16[768,512]{1,0:T(8,128)(2,1)S(1)}, u32[]{:S(2)}, u32[]{:S(2)}) collective-permute-start(bf16[768,512]{1,0:T(8,128)(2,1)} %fusion.112), channel_id=1, source_target_pairs={{8,16},{12,20},{16,8},{20,12},{9,17},{13,21},{17,9},{21,13},{10,18... | collective-permute-start | bytes 2359304 | tf_op jit(solution)/shard_map/ppermute | solution.py:179
  153.3 20.1 %collective-permute-start.27 = (bf16[768,512]{1,0:T(8,128)(2,1)}, bf16[768,512]{1,0:T(8,128)(2,1)S(1)}, u32[]{:S(2)}, u32[]{:S(2)}) collective-permute-start(bf16[768,512]{1,0:T(8,128)(2,1)} %fusion.112), channel_id=1, source_target_pairs={{8,0},{12,4},{16,24},{20,28},{9,1},{13,5},{17,25},{21,29},{10,2},{... | collective-permute-start | bytes 2359304 | tf_op jit(solution)/shard_map/ppermute | solution.py:179
  168.4 20.0 %collective-permute-start.30 = (bf16[768,512]{1,0:T(8,128)(2,1)S(1)}, bf16[768,512]{1,0:T(8,128)(2,1)S(1)}, u32[]{:S(2)}, u32[]{:S(2)}) collective-permute-start(bf16[768,512]{1,0:T(8,128)(2,1)S(1)} %add_convert_fusion.14), channel_id=1, source_target_pairs={{8,16},{12,20},{16,8},{20,12},{9,17},{13,21},{17,9},{21,13},{10,18... | collective-permute-start | bytes 2359304 | tf_op jit(solution)/shard_map/ppermute | solution.py:179
  187.0 16.7 %collective-permute-start.31 = (bf16[768,512]{1,0:T(8,128)(2,1)S(1)}, bf16[768,512]{1,0:T(8,128)(2,1)S(1)}, u32[]{:S(2)}, u32[]{:S(2)}) collective-permute-start(bf16[768,512]{1,0:T(8,128)(2,1)S(1)} %get-tuple-element.922), channel_id=1, source_target_pairs={{0,8},{4,12},{24,16},{28,20},{1,9},{5,13},{25,17},{29,21},{2,10},{... | collective-permute-start | bytes 2359304 | tf_op jit(solution)/shard_map/ppermute | solution.py:179
  193.3 17.7 %collective-permute-start.33 = (bf16[768,512]{1,0:T(8,128)(2,1)S(1)}, bf16[768,512]{1,0:T(8,128)(2,1)S(1)}, u32[]{:S(2)}, u32[]{:S(2)}) collective-permute-start(bf16[768,512]{1,0:T(8,128)(2,1)S(1)} %fusion.115), channel_id=1, source_target_pairs={{8,0},{12,4},{16,24},{20,28},{9,1},{13,5},{17,25},{21,29},{10,2},{... | collective-permute-start | bytes 2359304 | tf_op jit(solution)/shard_map/ppermute | solution.py:179
  194.6 34.3 %collective-permute-start.34 = (bf16[1536,512]{1,0:T(8,128)(2,1)S(1)}, bf16[1536,512]{1,0:T(8,128)(2,1)S(1)}, u32[]{:S(2)}, u32[]{:S(2)}) collective-permute-start(bf16[1536,512]{1,0:T(8,128)(2,1)S(1)} %convolution_convert_fusion.2), channel_id=1, source_target_pairs={{0,4},{4,0},{8,12},{12,8},{16,20},{20,16},{24,28},{28,24},{1,5},{5... | collective-permute-start | bytes 4718600 | tf_op jit(solution)/shard_map/ppermute | solution.py:179
  194.9 36.8 %collective-permute-start.35 = (bf16[768,512]{1,0:T(8,128)(2,1)S(1)}, bf16[768,512]{1,0:T(8,128)(2,1)S(1)}, u32[]{:S(2)}, u32[]{:S(2)}) collective-permute-start(bf16[768,512]{1,0:T(8,128)(2,1)S(1)} %get-tuple-element.968), channel_id=1, source_target_pairs={{0,8},{4,12},{24,16},{28,20},{1,9},{5,13},{25,17},{29,21},{2,10},{... | collective-permute-start | bytes 2359304 | tf_op jit(solution)/shard_map/ppermute | solution.py:179
  203.7 58.9 %collective-permute-start.40 = (bf16[512,1536]{1,0:T(8,128)(2,1)S(1)}, bf16[512,1536]{1,0:T(8,128)(2,1)S(1)}, u32[]{:S(2)}, u32[]{:S(2)}) collective-permute-start(bf16[512,1536]{1,0:T(8,128)(2,1)S(1)} %slice.231), channel_id=1, source_target_pairs={{0,4},{4,0},{8,12},{12,8},{16,20},{20,16},{24,28},{28,24},{1,5},{5... | collective-permute-start | bytes 4718600 | tf_op jit(solution)/shard_map/ppermute | solution.py:179
  204.2 27.5 %collective-permute-start.36 = (bf16[768,512]{1,0:T(8,128)(2,1)S(1)}, bf16[768,512]{1,0:T(8,128)(2,1)S(1)}, u32[]{:S(2)}, u32[]{:S(2)}) collective-permute-start(bf16[768,512]{1,0:T(8,128)(2,1)S(1)} %add_convert_fusion.11), channel_id=1, source_target_pairs={{8,16},{12,20},{16,8},{20,12},{9,17},{13,21},{17,9},{21,13},{10,18... | collective-permute-start | bytes 2359304 | tf_op jit(solution)/shard_map/ppermute | solution.py:179
  238.2 28.7 %collective-permute-start.41 = (bf16[768,512]{1,0:T(8,128)(2,1)S(1)}, bf16[768,512]{1,0:T(8,128)(2,1)S(1)}, u32[]{:S(2)}, u32[]{:S(2)}) collective-permute-start(bf16[768,512]{1,0:T(8,128)(2,1)S(1)} %collective-permute-done.26), channel_id=1, source_target_pairs={{8,0},{12,4},{16,24},{20,28},{9,1},{13,5},{17,25},{21,29},{10,2},{... | collective-permute-start | bytes 2359304 | tf_op jit(solution)/shard_map/ppermute | solution.py:179
  240.6 48.1 %collective-permute-start.42 = (bf16[768,512]{1,0:T(8,128)(2,1)S(1)}, bf16[768,512]{1,0:T(8,128)(2,1)S(1)}, u32[]{:S(2)}, u32[]{:S(2)}) collective-permute-start(bf16[768,512]{1,0:T(8,128)(2,1)S(1)} %collective-permute-done.32), channel_id=1, source_target_pairs={{8,0},{12,4},{16,24},{20,28},{9,1},{13,5},{17,25},{21,29},{10,2},{... | collective-permute-start | bytes 2359304 | tf_op jit(solution)/shard_map/ppermute | solution.py:179
  242.1 61.3 %collective-permute-start.44 = (bf16[768,512]{1,0:T(8,128)(2,1)S(1)}, bf16[768,512]{1,0:T(8,128)(2,1)S(1)}, u32[]{:S(2)}, u32[]{:S(2)}) collective-permute-start(bf16[768,512]{1,0:T(8,128)(2,1)S(1)} %get-tuple-element.1066), channel_id=1, source_target_pairs={{0,8},{4,12},{24,16},{28,20},{1,9},{5,13},{25,17},{29,21},{2,10},{... | collective-permute-start | bytes 2359304 | tf_op jit(solution)/shard_map/ppermute | solution.py:179
  250.3 53.2 %collective-permute-start.45 = (bf16[768,512]{1,0:T(8,128)(2,1)S(1)}, bf16[768,512]{1,0:T(8,128)(2,1)S(1)}, u32[]{:S(2)}, u32[]{:S(2)}) collective-permute-start(bf16[768,512]{1,0:T(8,128)(2,1)S(1)} %add_convert_fusion.8), channel_id=1, source_target_pairs={{8,16},{12,20},{16,8},{20,12},{9,17},{13,21},{17,9},{21,13},{10,18... | collective-permute-start | bytes 2359304 | tf_op jit(solution)/shard_map/ppermute | solution.py:179
  262.6 45.8 %collective-permute-start.47 = (bf16[768,512]{1,0:T(8,128)(2,1)S(1)}, bf16[768,512]{1,0:T(8,128)(2,1)S(1)}, u32[]{:S(2)}, u32[]{:S(2)}) collective-permute-start(bf16[768,512]{1,0:T(8,128)(2,1)S(1)} %collective-permute-done.38), channel_id=1, source_target_pairs={{8,0},{12,4},{16,24},{20,28},{9,1},{13,5},{17,25},{21,29},{10,2},{... | collective-permute-start | bytes 2359304 | tf_op jit(solution)/shard_map/ppermute | solution.py:179
  269.4 33.8 %collective-permute-start.43 = (bf16[1536,256]{1,0:T(8,128)(2,1)S(1)}, bf16[1536,256]{1,0:T(8,128)(2,1)S(1)}, u32[]{:S(2)}, u32[]{:S(2)}) collective-permute-start(bf16[1536,256]{1,0:T(8,128)(2,1)S(1)} %get-tuple-element.1235), channel_id=1, source_target_pairs={{0,1},{1,0},{2,3},{3,2},{4,5},{5,4},{6,7},{7,6},{8,9},{9,8},{10,11... | collective-permute-start | bytes 2359304 | tf_op jit(solution)/shard_map/ppermute | solution.py:179
  291.2 16.9 %collective-permute-start.46 = (bf16[1536,256]{1,0:T(8,128)(2,1)S(1)}, bf16[1536,256]{1,0:T(8,128)(2,1)S(1)}, u32[]{:S(2)}, u32[]{:S(2)}) collective-permute-start(bf16[1536,256]{1,0:T(8,128)(2,1)S(1)} %get-tuple-element.1233), channel_id=1, source_target_pairs={{0,1},{1,0},{2,3},{3,2},{4,5},{5,4},{6,7},{7,6},{8,9},{9,8},{10,11... | collective-permute-start | bytes 2359304 | tf_op jit(solution)/shard_map/ppermute | solution.py:179
  312.9 17.5 %collective-permute-start.50 = (bf16[1536,128]{1,0:T(8,128)(2,1)S(1)}, bf16[1536,128]{1,0:T(8,128)(2,1)S(1)}, u32[]{:S(2)}, u32[]{:S(2)}) collective-permute-start(bf16[1536,128]{1,0:T(8,128)(2,1)S(1)} %get-tuple-element.1241), channel_id=1, source_target_pairs={{0,2},{1,3},{2,0},{3,1},{4,6},{5,7},{6,4},{7,5},{8,10},{9,11},{10,... | collective-permute-start | bytes 1179656 | tf_op jit(solution)/shard_map/ppermute | solution.py:179
  313.2 23.8 %collective-permute-start.53 = (bf16[768,512]{1,0:T(8,128)(2,1)S(1)}, bf16[768,512]{1,0:T(8,128)(2,1)S(1)}, u32[]{:S(2)}, u32[]{:S(2)}) collective-permute-start(bf16[768,512]{1,0:T(8,128)(2,1)S(1)} %fusion.121), channel_id=1, source_target_pairs={{8,16},{12,20},{16,8},{20,12},{9,17},{13,21},{17,9},{21,13},{10,18... | collective-permute-start | bytes 2359304 | tf_op jit(solution)/shard_map/ppermute | solution.py:179
  313.9 24.4 %collective-permute-start.54 = (bf16[768,512]{1,0:T(8,128)(2,1)S(1)}, bf16[768,512]{1,0:T(8,128)(2,1)S(1)}, u32[]{:S(2)}, u32[]{:S(2)}) collective-permute-start(bf16[768,512]{1,0:T(8,128)(2,1)S(1)} %fusion.121), channel_id=1, source_target_pairs={{8,0},{12,4},{16,24},{20,28},{9,1},{13,5},{17,25},{21,29},{10,2},{... | collective-permute-start | bytes 2359304 | tf_op jit(solution)/shard_map/ppermute | solution.py:179
  315.5 25.8 %collective-permute-start.55 = (bf16[1536,128]{1,0:T(8,128)(2,1)S(1)}, bf16[1536,128]{1,0:T(8,128)(2,1)S(1)}, u32[]{:S(2)}, u32[]{:S(2)}) collective-permute-start(bf16[1536,128]{1,0:T(8,128)(2,1)S(1)} %get-tuple-element.1239), channel_id=1, source_target_pairs={{0,2},{1,3},{2,0},{3,1},{4,6},{5,7},{6,4},{7,5},{8,10},{9,11},{10,... | collective-permute-start | bytes 1179656 | tf_op jit(solution)/shard_map/ppermute | solution.py:179
  338.3 25.2 %collective-permute-start.62 = (bf16[768,512]{1,0:T(8,128)(2,1)S(1)}, bf16[768,512]{1,0:T(8,128)(2,1)S(1)}, u32[]{:S(2)}, u32[]{:S(2)}) collective-permute-start(bf16[768,512]{1,0:T(8,128)(2,1)S(1)} %collective-permute-done.53), channel_id=1, source_target_pairs={{8,0},{12,4},{16,24},{20,28},{9,1},{13,5},{17,25},{21,29},{10,2},{... | collective-permute-start | bytes 2359304 | tf_op jit(solution)/shard_map/ppermute | solution.py:179
  (69 other events, 636.6 us)
